TPU v7x, 32 devices: a whole 2x2x4 slice. The times are simulated.
32 devices in a mesh: row: 4 (over x, core), col: 8 (over z, y).
Axes of the slice: x: 2, y: 2, z: 4, core: 2. Of those that a mesh axis runs over, the one named last changes fastest.
Arguments:
- tile_feats: bfloat16 [32, 32, 128, 192], P(('row', 'col')), may hold values from -6 to 6
- tile_cell: int32 [32, 32, 128], P(('row', 'col')), may hold values from 0 to 4095, as said below
- tile_mask: int32 [32, 32, 128], P(('row', 'col')), may hold values 0 or 1
- tile_count: int32 [32, 32], P(('row', 'col')), may hold values from 0 to 128, as said below
- background: bfloat16 [192], replicated, may hold values from -6 to 6
- norm_gain: float32 [192], replicated, may hold values from 0.1 to 1.9
- in_x: bfloat16 [192, 384], replicated, may hold values from -0.4375 to 0.4375
- in_z: bfloat16 [192, 384], replicated, may hold values from -0.4375 to 0.4375
- conv_w: float32 [3, 3, 384], replicated, may hold values from -2 to 2
- conv_bias: float32 [384], replicated, may hold values from -3 to 3
- x_proj: bfloat16 [384, 128], replicated, may hold values from -0.15625 to 0.15625
- skip_gain: float32 [384], replicated, may hold values from 0.5 to 1.5
- decay_rate: float32 [4, 6, 128, 1024], P(None, None, 'row', 'col'), may hold values from 0 to 1
- out_gain: float32 [384], replicated, may hold values from 0.1 to 1.9
- out_w: bfloat16 [384, 192], replicated, may hold values from -0.3125 to 0.3125
- mlp_gain: float32 [192], replicated, may hold values from 0.1 to 1.9
- ff_in: bfloat16 [192, 768], replicated, may hold values from -0.4375 to 0.4375
- ff_out: bfloat16 [768, 192], replicated, may hold values from -0.21875 to 0.21875
Outputs:
- block_out: bfloat16 [128, 1024, 192], P('row', 'col')
Inputs may be any that keep to these rules, and one draw needn't show every extreme that they name: `tile_cell`: cells of the owner's block of 32 x 128 cells, numbered row by row; the live slots sent to one owner by all loaders name distinct cells. `tile_count`: the live slots from a loader to an owner are its first ones; some owner receives 128 from every loader.
All inputs are finite; a program needn't handle non-finite values. No bound on the sum of `tile_mask` on one device may be relied on, other than what follows from the above.
Results may differ from a plain program's by a relative error of at most 0.015.
Values may be sent and summed in bfloat16 or wider, within the bound.
A program may use at most 384 MiB of HBM per device.

v0:
```python
import jax
import jax.numpy as jnp
from jax import lax
from jax.sharding import PartitionSpec as P


def prefix(shard, axis, combine, identity, reverse):
    peers, index = (lax.axis_size(axis), lax.axis_index(axis))
    everything = jax.tree.map(
        lambda part, kind: lax.all_gather(part.astype(kind), axis),
        shard,
        (jnp.bfloat16, jnp.bfloat16),
    )
    start = jax.tree.map(
        lambda part, zero: jnp.broadcast_to(jnp.asarray(zero, part.dtype), part.shape),
        shard,
        identity,
    )

    def hop(k, before):
        at = peers - 1 - k if reverse else k
        reached = at > index if reverse else at < index
        new = combine(
            before, jax.tree.map(lambda part, own: part[at].astype(own.dtype), everything, shard)
        )
        return jax.tree.map(lambda a, b: jnp.where(reached, a, b), new, before)

    return lax.fori_loop(0, peers, hop, start)


def padded_2(block, sides, width):
    for axis, dim in sides:
        count = lax.axis_size(axis)
        forward = [(i, i + 1) for i in range(count - 1)]
        backward = [(target, source) for source, target in forward]
        low = lax.ppermute(
            lax.slice_in_dim(block, block.shape[dim] - width, None, axis=dim), axis, forward
        )
        high = lax.ppermute(lax.slice_in_dim(block, 0, width, axis=dim), axis, backward)
        block = jnp.concatenate([low, block, high], axis=dim)
    return block


def rms_scale(values, gains):
    return values * lax.rsqrt(jnp.mean(values * values, axis=-1, keepdims=True) + 1e-06) * gains


def block_parts(x_vals, b_coef, c_coef, rates):
    cumulative = jnp.cumsum(rates, axis=2)
    weight = jnp.sqrt(-jnp.expm1(-2.0 * rates))
    scaled = x_vals.astype(jnp.float32) * jnp.swapaxes(weight, 1, 2)[..., None]
    scores = jnp.einsum("stn,sun->stu", c_coef, b_coef, preferred_element_type=jnp.float32)
    length = rates.shape[2]
    causal = lax.broadcasted_iota(jnp.int32, (length, length), 0) >= lax.broadcasted_iota(
        jnp.int32, (length, length), 1
    )
    log_gap = cumulative[:, :, :, None] - cumulative[:, :, None, :]
    mixing = jnp.where(causal, jnp.exp(-jnp.maximum(log_gap, 0.0)), 0.0) * scores[:, None]
    inner_part = jnp.einsum("shtu,suhp->sthp", mixing, scaled, precision=lax.Precision.HIGHEST)
    to_end = jnp.exp(cumulative - cumulative[:, :, -1:])
    weighted = scaled * jnp.swapaxes(to_end, 1, 2)[..., None]
    final_state = jnp.einsum(
        "suhp,sun->shpn", weighted, b_coef.astype(jnp.float32), precision=lax.Precision.HIGHEST
    )
    total_decay = jnp.exp(-cumulative[:, :, -1])
    return (inner_part, final_state, total_decay, cumulative)


def blocked_parts(x_vals, b_coef, c_coef, rates):
    sequences = x_vals.shape[0]
    groups = sequences // 16

    def grouped(array):
        return array.reshape((groups, 16) + array.shape[1:])

    def ungrouped(array):
        return array.reshape((sequences,) + array.shape[2:])

    parts = lax.map(
        lambda block_args: block_parts(*block_args),
        (grouped(x_vals), grouped(b_coef), grouped(c_coef), grouped(rates)),
    )
    return tuple((ungrouped(array) for array in parts))


def carry_part(c_coef, cumulative, entering):
    reached = jnp.einsum(
        "stn,shpn->sthp", c_coef.astype(jnp.float32), entering, precision=lax.Precision.HIGHEST
    )
    return reached * jnp.swapaxes(jnp.exp(-cumulative), 1, 2)[..., None]


def pass_carry(direction, total_decay, final_state):

    def combine(earlier, latter):
        return (earlier[0] * latter[0], latter[0][..., None, None] * earlier[1] + latter[1])

    neutral = (jnp.ones_like(total_decay), jnp.zeros_like(final_state))
    if direction == 0:
        passed = prefix((total_decay, final_state), "col", combine, neutral, False)
    elif direction == 1:
        passed = prefix((total_decay, final_state), "col", combine, neutral, True)
    elif direction == 2:
        passed = prefix((total_decay, final_state), "row", combine, neutral, False)
    else:
        passed = prefix((total_decay, final_state), "row", combine, neutral, True)
    return passed[1]


def orient(direction, scan_in, coeffs, rate_all):
    rows_n, cols_n, width = scan_in.shape
    head_count = rate_all.shape[1]
    state_size = coeffs.shape[2] // 8
    x_vals = scan_in.reshape(rows_n, cols_n, head_count, width // head_count)
    b_coef = coeffs[:, :, 2 * direction * state_size : (2 * direction + 1) * state_size]
    c_coef = coeffs[:, :, (2 * direction + 1) * state_size : (2 * direction + 2) * state_size]
    rates = rate_all[direction]
    if direction >= 2:
        x_vals = jnp.swapaxes(x_vals, 0, 1)
        b_coef = jnp.swapaxes(b_coef, 0, 1)
        c_coef = jnp.swapaxes(c_coef, 0, 1)
        rates = jnp.transpose(rates, (2, 0, 1))
    else:
        rates = jnp.transpose(rates, (1, 0, 2))
    if direction % 2 == 1:
        x_vals = jnp.flip(x_vals, 1)
        b_coef = jnp.flip(b_coef, 1)
        c_coef = jnp.flip(c_coef, 1)
        rates = jnp.flip(rates, 2)
    return (x_vals, b_coef, c_coef, rates)


def restore(direction, result, rows_n, cols_n):
    if direction % 2 == 1:
        result = jnp.flip(result, 1)
    if direction >= 2:
        result = jnp.swapaxes(result, 0, 1)
    return result.reshape(rows_n, cols_n, -1)


def sharded_direction(direction, scan_in, coeffs, decay_rate):
    rows_n, cols_n = (scan_in.shape[0], scan_in.shape[1])
    x_vals, b_coef, c_coef, rates = orient(direction, scan_in, coeffs, decay_rate)
    inner_part, final_state, total_decay, cumulative = blocked_parts(x_vals, b_coef, c_coef, rates)
    entering = pass_carry(direction, total_decay, final_state)
    result = inner_part + carry_part(c_coef, cumulative, entering)
    return restore(direction, result, rows_n, cols_n)


def local(
    tile_feats,
    tile_cell,
    tile_mask,
    tile_count,
    background,
    norm_gain,
    in_x,
    in_z,
    conv_w,
    conv_bias,
    x_proj,
    skip_gain,
    decay_rate,
    out_gain,
    out_w,
    mlp_gain,
    ff_in,
    ff_out,
):
    rows_n, cols_n = (decay_rate.shape[2], decay_rate.shape[3])
    channels = tile_feats.shape[3]
    slots = tile_feats.shape[2]
    width = in_x.shape[1]
    values = jnp.where(tile_mask[..., None] == 1, tile_feats, background)
    slot_live = jnp.arange(slots, dtype=jnp.int32)[None, None, :] < tile_count[:, :, None]
    marked = jnp.where(slot_live, tile_cell, rows_n * cols_n)
    got_values, got_cells = (
        lax.all_to_all(values, ("row", "col"), split_axis=1, concat_axis=0, tiled=True),
        lax.all_to_all(marked, ("row", "col"), split_axis=1, concat_axis=0, tiled=True),
    )
    tile_grid = (
        jnp.zeros((rows_n * cols_n + 1, channels), jnp.bfloat16)
        .at[got_cells.reshape(-1)]
        .set(got_values.reshape(-1, channels))
    )
    tile_grid = tile_grid[:-1].reshape(rows_n, cols_n, channels)
    normed = rms_scale(tile_grid.astype(jnp.float32), norm_gain).astype(jnp.bfloat16)
    inner_x = jnp.dot(normed, in_x, preferred_element_type=jnp.float32).astype(jnp.bfloat16)
    padded = padded_2(inner_x, (("row", 0), ("col", 1)), 1)
    gate_out = jnp.dot(normed, in_z, preferred_element_type=jnp.float32).astype(jnp.bfloat16)
    summed_conv = jnp.zeros((rows_n, cols_n, width), jnp.float32) + conv_bias
    for shift_row in range(3):
        for shift_col in range(3):
            summed_conv = (
                summed_conv
                + padded[shift_row : shift_row + rows_n, shift_col : shift_col + cols_n].astype(
                    jnp.float32
                )
                * conv_w[shift_row, shift_col]
            )
    scan_in = jax.nn.silu(summed_conv).astype(jnp.bfloat16)
    coeffs = jnp.dot(scan_in, x_proj, preferred_element_type=jnp.float32).astype(jnp.bfloat16)
    summed = skip_gain * scan_in.astype(jnp.float32)
    for direction in range(2):
        summed = summed + sharded_direction(direction, scan_in, coeffs, decay_rate)
    for direction in range(2, 4):
        summed = summed + sharded_direction(direction, scan_in, coeffs, decay_rate)
    gated_out = (rms_scale(summed, out_gain) * jax.nn.silu(gate_out.astype(jnp.float32))).astype(
        jnp.bfloat16
    )
    middle = (
        jnp.dot(gated_out, out_w, preferred_element_type=jnp.float32)
        + tile_grid.astype(jnp.float32)
    ).astype(jnp.bfloat16)
    normed_mid = rms_scale(middle.astype(jnp.float32), mlp_gain).astype(jnp.bfloat16)
    hidden = jax.nn.gelu(
        jnp.dot(normed_mid, ff_in, preferred_element_type=jnp.float32), approximate=False
    ).astype(jnp.bfloat16)
    return (
        jnp.dot(hidden, ff_out, preferred_element_type=jnp.float32) + middle.astype(jnp.float32)
    ).astype(jnp.bfloat16)


def solution(mesh):
    placed = (
        P(("row", "col"), None, None, None),
        P(("row", "col"), None, None),
        P(("row", "col"), None, None),
        P(("row", "col"), None),
        P(),
        P(),
        P(),
        P(),
        P(),
        P(),
        P(),
        P(),
        P(None, None, "row", "col"),
        P(),
        P(),
        P(),
        P(),
        P(),
    )
    return jax.shard_map(
        local, mesh=mesh, in_specs=placed, out_specs=P("row", "col", None), check_vma=False
    )
```

profile of v0, /device:TPU:0, one launch (start us, length us, event | category | flops | bytes accessed | tf_op | source)
XLA Modules:
  0.0 936.9 jit_solution(12254781010403477863)
XLA Ops:
  8.0 7.3 all-to-all-start
  25.2 38.8 %all-to-all-done.1 = bf16[1,32,128,192]{2,3,0,1:T(8,128)(2,1)S(1)} async-done(((bf16[1,32,128,192]{2,3,0,1:T(8,128)(2,1)}), bf16[1,32,128,192]{2,3,0,1:T(8,128)(2,1)S(1)}, u32[]{:S(2)}, u32[]{:S(2)}) %all-to-all-start.1) | async-done | bytes 1572896 | tf_op jit(solution)/shard_map/all_to_all | solution.py:178
  66.6 18.8 %scatter_custom_fusion = bf16[4097,192]{1,0:T(8,128)(2,1)S(1)} fusion(s32[4096]{0:T(1024)S(1)} %bitcast.481, bf16[4096,192]{1,0:T(8,128)(2,1)} %bitcast.463, bf16[]{:T(256)} %constant.284.clone.1), kind=kCustom, calls=%fused_computation.250 | custom fusion | bytes 1573760 | tf_op jit(solution)/shard_map/scatter | solution.py:184
  115.0 12.0 %multiply_convert_fusion = bf16[32,128,384]{2,1,0:T(8,128)(2,1)} fusion(bf16[32,128,384]{2,1,0:T(8,128)(2,1)S(1)} %convolution_convert_fusion, bf16[34,129,384]{2,1,0:T(8,128)(2,1)S(1)} %get-tuple-element.1056, bf16[1,128,384]{2,1,0:T(8,128)(2,1)S(1)} %copy-done.13, bf16[34,129,384]{2,1,0:T(8,128)(2,1)S(1)} %get-tuple-element.1055, ...), kind=kLoop, calls=%fused_computation.221 | loop fusion | flops 53477376 | bytes 25377792 | tf_op jit(solution)/shard_map/convert_element_type | solution.py:201
  136.6 5.5 rev.38
  147.7 43.3 %while.125 = (s32[]{:T(128)}, f32[2,16,128,6,64]{2,4,3,1,0:T(8,128)}, bf16[2,16,6,64,16]{3,4,2,1,0:T(8,128)(2,1)S(1)}, bf16[2,16,6]{1,0,2:T(2,128)(2,1)S(1)}, f3...) while((s32[]{:T(128)}, ...), condition=%wide.region_9.10_spmd, body=%wide.region_7.9_spmd.sunk | while | flops 1380753536 | bytes 22664936 | solution.py:79
  150.1 15.1 %bitcast_dynamic-update-slice_fusion.18 = f32[2,16,128,6,64]{2,4,3,1,0:T(8,128)} fusion(f32[2,16,128,6,64]{2,4,3,1,0:T(8,128)} %get-tuple-element.1586, s32[]{:T(128)S(6)} %copy.364, f32[16,128,128]{2,1,0:T(8,128)S(1)} %fusion.306, f32[16,6,128]{2,1,0:T(8,128)S(1)} %copy.290, pred[128,128]{1,0:T(8,128)(4,1)S(1)} %iota_compare_fusion.9, ...), kind=kOutput, calls=%fused_computation.65.clone.1 | convolution fusion | flops 1217396736 | bytes 5981184 | tf_op jit(solution)/shard_map/while/body/eval_jaxpr/shtu,suhp->sthp/dot_general | solution.py:59
  171.7 15.1 %bitcast_dynamic-update-slice_fusion.18 = f32[2,16,128,6,64]{2,4,3,1,0:T(8,128)} fusion(f32[2,16,128,6,64]{2,4,3,1,0:T(8,128)} %get-tuple-element.1586, s32[]{:T(128)S(6)} %copy.364, f32[16,128,128]{2,1,0:T(8,128)S(1)} %fusion.306, f32[16,6,128]{2,1,0:T(8,128)S(1)} %copy.290, pred[128,128]{1,0:T(8,128)(4,1)S(1)} %iota_compare_fusion.9, ...), kind=kOutput, calls=%fused_computation.65.clone.1 | convolution fusion | flops 1217396736 | bytes 5981184 | tf_op jit(solution)/shard_map/while/body/eval_jaxpr/shtu,suhp->sthp/dot_general | solution.py:59
  200.1 5.5 copy.232
  205.6 4.7 rev.43
  210.3 10.3 %copy.219 = bf16[128,32,6,64]{3,1,2,0:T(8,128)(2,1)} copy(bf16[128,32,6,64]{0,3,2,1:T(8,128)(2,1)} %rev.43) | data formatting | bytes 6291456 | tf_op jit(solution)/shard_map/jit(_flip)/rev | solution.py:126
  233.1 56.1 %while.124 = (s32[]{:T(128)}, f32[2,16,128,6,64]{2,4,3,1,0:T(8,128)}, bf16[2,16,6,64,16]{3,4,2,1,0:T(8,128)(2,1)}, bf16[2,16,6]{1,0,2:T(2,128)(2,1)S(1)}, f32[2,...) while((s32[]{:T(128)}, ...), condition=%wide.region_4.5_spmd, body=%wide.region_2.4_spmd.sunk | while | flops 1380753536 | bytes 26335036 | solution.py:79
  240.1 15.3 %bitcast_dynamic-update-slice_fusion.16 = f32[2,16,128,6,64]{2,4,3,1,0:T(8,128)} fusion(f32[2,16,128,6,64]{2,4,3,1,0:T(8,128)} %get-tuple-element.1649, s32[]{:T(128)S(6)} %copy.385, f32[16,128,128]{2,1,0:T(8,128)} %fusion.299, f32[16,6,128]{2,1,0:T(8,128)S(1)} %copy.287, pred[128,128]{1,0:T(8,128)(4,1)S(1)} %iota_compare_fusion.8, ...), kind=kOutput, calls=%fused_computation.22.clone.1 | convolution fusion | flops 1217396736 | bytes 5981184 | tf_op jit(solution)/shard_map/while/body/eval_jaxpr/shtu,suhp->sthp/dot_general | solution.py:59
  268.1 15.3 %bitcast_dynamic-update-slice_fusion.16 = f32[2,16,128,6,64]{2,4,3,1,0:T(8,128)} fusion(f32[2,16,128,6,64]{2,4,3,1,0:T(8,128)} %get-tuple-element.1649, s32[]{:T(128)S(6)} %copy.385, f32[16,128,128]{2,1,0:T(8,128)} %fusion.299, f32[16,6,128]{2,1,0:T(8,128)S(1)} %copy.287, pred[128,128]{1,0:T(8,128)(4,1)S(1)} %iota_compare_fusion.8, ...), kind=kOutput, calls=%fused_computation.22.clone.1 | convolution fusion | flops 1217396736 | bytes 5981184 | tf_op jit(solution)/shard_map/while/body/eval_jaxpr/shtu,suhp->sthp/dot_general | solution.py:59
  289.3 6.1 broadcast.199.clone
  298.3 118.4 %while.127 = (s32[]{:T(128)}, f32[8,16,32,6,64]{4,2,3,1,0:T(8,128)}, bf16[8,16,6,64,16]{3,4,2,1,0:T(8,128)(2,1)}, bf16[8,16,6]{1,0,2:T(8,128)(2,1)S(1)}, f32[8,1...) while((s32[]{:T(128)}, f32[8,16,32,6,64]{4,2,3,1,0:T(8,128)}, ...), condition=%wide.region_19.20_spmd, body=%wide.region_17.19_spmd.sunk | while | flops 115350624 | bytes 4909773 | solution.py:79
  304.5 4.6 bitcast_dynamic-update-slice_fusion.22
  319.3 4.5 bitcast_dynamic-update-slice_fusion.22
  334.0 4.6 bitcast_dynamic-update-slice_fusion.22
  348.9 4.6 bitcast_dynamic-update-slice_fusion.22
  363.7 4.6 bitcast_dynamic-update-slice_fusion.22
  378.5 4.6 bitcast_dynamic-update-slice_fusion.22
  393.3 4.6 bitcast_dynamic-update-slice_fusion.22
  408.1 4.5 bitcast_dynamic-update-slice_fusion.22
  416.7 10.3 %copy.207 = bf16[128,32,6,64]{3,1,2,0:T(8,128)(2,1)} copy(bf16[128,32,6,64]{0,3,2,1:T(8,128)(2,1)} %bitcast.447) | data formatting | bytes 6291456 | tf_op jit(solution)/shard_map/transpose | solution.py:119
  433.6 6.5 copy.224
  444.6 6.2 broadcast.199.clone.1
  453.8 118.4 %while.126 = (s32[]{:T(128)}, f32[8,16,32,6,64]{4,2,3,1,0:T(8,128)}, bf16[8,16,6,64,16]{3,4,2,1,0:T(8,128)(2,1)}, bf16[8,16,6]{1,0,2:T(8,128)(2,1)S(1)}, f32[8,1...) while((s32[]{:T(128)}, f32[8,16,32,6,64]{4,2,3,1,0:T(8,128)}, ...), condition=%wide.region_14.15_spmd, body=%wide.region_12.14_spmd.sunk | while | flops 115350624 | bytes 4909773 | solution.py:79
  460.1 4.5 bitcast_dynamic-update-slice_fusion.20
  474.9 4.5 bitcast_dynamic-update-slice_fusion.20
  504.4 4.6 bitcast_dynamic-update-slice_fusion.20
  519.2 4.5 bitcast_dynamic-update-slice_fusion.20
  534.0 4.6 bitcast_dynamic-update-slice_fusion.20
  548.8 4.6 bitcast_dynamic-update-slice_fusion.20
  577.2 6.5 copy.212
  587.0 26.0 %all_gather.34 = bf16[8,32,6]{1,2,0:T(8,128)(2,1)S(1)} all-gather(bf16[1,32,6]{1,2,0:T(8,128)(2,1)S(1)} %convert_element_type.343), channel_id=1, replica_groups=mesh['row'=4,'col'=8] {'col'}, dimensions={0}, use_global_device_ids=true | all-gather | bytes 3456 | tf_op jit(solution)/shard_map/all_gather | solution.py:10
  613.0 26.0 %all_gather.32 = bf16[8,32,6]{1,2,0:T(8,128)(2,1)S(1)} all-gather(bf16[1,32,6]{1,2,0:T(8,128)(2,1)S(1)} %convert_element_type.339), channel_id=1, replica_groups=mesh['row'=4,'col'=8] {'col'}, dimensions={0}, use_global_device_ids=true | all-gather | bytes 3456 | tf_op jit(solution)/shard_map/all_gather | solution.py:10
  639.0 7.7 all_gather.38
  646.6 5.6 all_gather.36
  652.3 27.1 %while.129 = (s32[]{:T(128)}, f32[32,6,64,16]{2,3,1,0:T(8,128)}, s32[]{:T(128)}, bf16[8,32,6]{1,2,0:T(8,128)(2,1)S(1)}, bf16[8,32,6,64,16]{3,4,2,1,0:T(8,128)(2,...) while((s32[]{:T(128)}, f32[32,6,64,16]{2,3,1,0:T(8,128)}, s32[]{:T(128)}, ...), condition=%wide.region_11.12_spmd.clone, body=%wide.region_10.11_spmd.clone.sunk | while | flops 983240 | bytes 1969711 | solution.py:28
  679.4 9.3 bitcast_add_fusion.2
  688.7 10.2 %rev.42 = f32[32,128,6,64]{1,3,2,0:T(8,128)} reverse(f32[32,128,6,64]{1,3,2,0:T(8,128)} %bitcast_add_fusion.2), dimensions={1} | reverse | bytes 12582912 | tf_op jit(solution)/shard_map/jit(_flip)/rev | solution.py:135
  698.9 6.5 copy.206
  705.5 26.0 %while.128 = (s32[]{:T(128)}, f32[32,6,64,16]{2,3,1,0:T(8,128)}, s32[]{:T(128)}, bf16[8,32,6]{1,2,0:T(8,128)(2,1)S(1)}, bf16[8,32,6,64,16]{3,4,2,1,0:T(8,128)(2,1)}, /*index=5*/s32[]{:T(128)}, s32[]{:T(128)}) while((s32[]{:T(128)}, f32[32,6,64,16]{2,3,1,0:T(8,128)}, s32[]{:T(128)}, bf16[8,32,6]{1,2,0:T(8,128)(2,1)S(1)}, ...), condition=%wide.region_6.7_spmd.clone, body=%wide.region_5.6_spmd.clone.sunk | while | flops 983236 | bytes 1969649 | solution.py:28
  731.5 9.3 bitcast_add_fusion.3
  740.8 6.5 copy.200
  747.3 17.2 %while.131 = (s32[]{:T(128)}, f32[128,6,64,16]{0,3,2,1:T(8,128)}, s32[]{:T(128)}, bf16[4,128,6]{1,2,0:T(8,128)(2,1)S(1)}, bf16[4,128,6,64,16]{1,4,3,2,0:T(8,128)...) while((s32[]{:T(128)}, f32[128,6,64,16]{0,3,2,1:T(8,128)}, s32[]{:T(128)}, ...), condition=%wide.region_21.22_spmd.clone, body=%wide.region_20.21_spmd.clone.sunk | while | flops 3932936 | bytes 7872175 | solution.py:28
  750.9 4.5 fusion.325
  755.5 4.5 fusion.325
  760.0 4.5 fusion.325
  764.5 7.5 copy.226
  772.1 16.0 %bitcast_add_fusion = f32[128,32,6,64]{3,1,2,0:T(8,128)} fusion(f32[8,16,32,6,64]{4,2,3,1,0:T(8,128)} %get-tuple-element.672, f32[128,32,6]{1,2,0:T(8,128)} %copy.228, bf16[128,32,16,1]{1,2,3,0:T(8,128)(2,1)} %copy.241, f32[128,6,64,16]{2,3,1,0:T(8,128)} %copy.226), kind=kOutput, calls=%fused_computation.196 | convolution fusion | flops 305135616 | bytes 15958016 | tf_op jit(solution)/shard_map/stn,shpn->sthp/dot_general | solution.py:87
  788.1 17.3 %rev.47 = f32[128,32,6,64]{3,1,2,0:T(8,128)} reverse(f32[128,32,6,64]{3,1,2,0:T(8,128)} %bitcast_add_fusion), dimensions={1} | reverse | bytes 12582912 | tf_op jit(solution)/shard_map/jit(_flip)/rev | solution.py:135
  805.4 11.5 %copy.229 = f32[32,128,6,64]{1,3,2,0:T(8,128)} copy(f32[32,128,6,64]{3,0,2,1:T(8,128)} %bitcast.443) | data formatting | bytes 12582912 | tf_op jit(solution)/shard_map/transpose | solution.py:137
  816.8 6.6 copy.230
  823.5 13.5 %while.130 = (s32[]{:T(128)}, f32[128,6,64,16]{0,3,2,1:T(8,128)S(1)}, s32[]{:T(128)}, bf16[4,128,6]{1,2,0:T(8,128)(2,1)S(1)}, bf16[4,128,6,64,16]{1,4,3,2,0:T(8,128)(2,1)}, /*index=5*/s32[]{:T(128)}, s32[]{:T(128)}) while((s32[]{:T(128)}, f32[128,6,64,16]{0,3,2,1:T(8,128)S(1)}, s32[]{:T(128)}, ...), condition=%wide.region_16.17_spmd.clone, body=%wide.region_15.16_spmd.clone.sunk | while | flops 3932932 | bytes 7872113 | solution.py:28
  837.0 6.1 copy.214
  843.1 16.2 %fusion.184 = f32[32,128,6,64]{3,0,2,1:T(8,128)} fusion(f32[128,32,6]{1,2,0:T(8,128)} %copy.216, bf16[128,32,16,1]{1,2,3,0:T(8,128)(2,1)} %copy.240, f32[128,6,64,16]{2,3,1,0:T(8,128)} %copy.214, f32[8,16,32,6,64]{4,2,3,1,0:T(8,128)} %get-tuple-element.667), kind=kOutput, calls=%fused_computation.227 | convolution fusion | flops 305135616 | bytes 15958016 | tf_op jit(solution)/shard_map/stn,shpn->sthp/dot_general | solution.py:87
  859.3 11.3 %copy.217 = f32[32,128,6,64]{1,3,2,0:T(8,128)} copy(f32[32,128,6,64]{3,0,2,1:T(8,128)} %fusion.184) | data formatting | bytes 12582912 | tf_op jit(solution)/shard_map/transpose | solution.py:137
  870.6 6.8 copy.218
  877.4 12.0 %multiply_reduce_fusion = (f32[32,128]{1,0:T(8,128)S(1)}, f32[32,128,384]{2,1,0:T(8,128)}) fusion(f32[32,128,384]{2,1,0:T(8,128)} %copy.230, f32[32,128,384]{2,1,0:T(8,128)} %copy.218, f32[32,128,384]{2,1,0:T(8,128)} %copy.206, f32[32,128,384]{2,1,0:T(8,128)} %copy.200, bf16[32,128,384]{2,1,0:T(8,128)(2,1)S(1)} %copy-done.3, f32[384]{0:T(512)S(1)} %copy-done.26), kind=kLoop, calls=%fused_computation.219 | loop fusion | flops 12578816 | bytes 34620928 | tf_op jit(solution)/shard_map/reduce_sum | solution.py:45
  889.4 6.7 fusion.185
  896.1 4.9 convert_reduce_fusion.1
  901.0 29.1 %fusion.188 = bf16[32,128,192]{1,2,0:T(8,128)(2,1)} fusion(bf16[32,128,192]{1,2,0:T(8,128)(2,1)S(1)} %get-tuple-element.1075, f32[32,128,768]{2,1,0:T(8,128)S(1)} %get-tuple-element.1076, u32[128,768]{1,0:T(8,128)S(1)} %get-tuple-element.923, u32[128,768]{1,0:T(8,128)S(1)} %get-tuple-element.922, bf16[768,192]{0,1:T(8,128)(2,1)S(1)} %copy-done.28), kind=kOutput, calls=%fused_computation.234 | convolution fusion | flops 1424228352 | bytes 16809984 | tf_op jit(solution)/shard_map/dot_general | solution.py:220
  (501 shorter events, 384.9 us)
Async XLA Ops:
  6.5 889.5 %copy-start = (bf16[192,768]{1,0:T(8,128)(2,1)S(1)}, bf16[192,768]{1,0:T(8,128)(2,1)}, u32[]{:S(2)}) copy-start(bf16[192,768]{1,0:T(8,128)(2,1)} %param.50) | copy-start | bytes 884740
  8.0 14.4 %all-to-all-start = ((s32[1,32,128]{2,0,1:T(1,128)}), s32[1,32,128]{2,0,1:T(1,128)S(1)}, u32[]{:S(2)}, u32[]{:S(2)}) async-start(s32[1,32,128]{2,0,1:T(1,128)} %compare_select_fusion.1), calls=%async_computation | async-start | bytes 32768 | tf_op jit(solution)/shard_map/all_to_all | solution.py:179
  22.4 41.5 %all-to-all-start.1 = ((bf16[1,32,128,192]{2,3,0,1:T(8,128)(2,1)}), bf16[1,32,128,192]{2,3,0,1:T(8,128)(2,1)S(1)}, u32[]{:S(2)}, u32[]{:S(2)}) async-start(bf16[1,32,128,192]{2,3,0,1:T(8,128)(2,1)} %bitcast_select_fusion), calls=%async_computation.1 | async-start | bytes 3145728 | tf_op jit(solution)/shard_map/all_to_all | solution.py:178
  25.1 627.1 %all-gather.7.cloned.1.call-start = ((), (), s32[]{:S(2)}) async-start(), calls=%async_computation.3 | async-start | bytes 7077888 | tf_op jit(solution)/shard_map/all_gather | solution.py:10
  87.7 4.5 copy-start.27
  92.2 8.3 copy-start.16
  92.3 14.8 %copy-start.20 = (f32[3,3,384]{2,1,0:T(4,128)S(1)}, f32[3,3,384]{2,1,0:T(4,128)}, u32[]{:S(2)}) copy-start(f32[3,3,384]{2,1,0:T(4,128)} %param.42) | copy-start | bytes 41476
  92.7 1.2 copy-start.4
  96.2 5.1 collective-permute-start.1
  97.5 4.0 collective-permute-start
  101.3 0.6 copy-start.12
  102.0 0.7 copy-start.14
  102.7 6.1 collective-permute-start.2
  105.6 6.3 collective-permute-start.3
  108.7 6.2 copy-start.13
  108.7 6.2 copy-start.15
  108.7 6.2 copy-start.21
  108.7 6.2 copy-start.22
  108.8 6.2 copy-start.23
  108.8 6.2 copy-start.24
  108.8 6.2 copy-start.25
  130.4 11.7 %copy-start.1 = (bf16[32,128,384]{1,2,0:T(8,128)(2,1)}, bf16[32,128,384]{1,2,0:T(8,128)(2,1)S(1)}, u32[]{:S(2)}) copy-start(bf16[32,128,384]{1,2,0:T(8,128)(2,1)S(1)} %copy.194) | copy-start | bytes 9437188
  134.6 1.0 copy-start.5
  150.1 15.4 %copy-start.6 = (bf16[2,16,128,6,64]{2,4,3,1,0:T(8,128)(2,1)S(1)}, bf16[2,16,128,6,64]{2,4,3,1,0:T(8,128)(2,1)}, u32[]{:S(2)}) copy-start(bf16[2,16,128,6,64]{2,4,3,1,0:T(8,128)(2,1)} %get-tuple-element.1602) | copy-start | bytes 9437188 | tf_op jit(solution)/shard_map/while
  171.7 15.4 %copy-start.6 = (bf16[2,16,128,6,64]{2,4,3,1,0:T(8,128)(2,1)S(1)}, bf16[2,16,128,6,64]{2,4,3,1,0:T(8,128)(2,1)}, u32[]{:S(2)}) copy-start(bf16[2,16,128,6,64]{2,4,3,1,0:T(8,128)(2,1)} %get-tuple-element.1602) | copy-start | bytes 9437188 | tf_op jit(solution)/shard_map/while
  191.0 0.9 copy-start.7
  191.0 1.0 copy-start.10
  191.0 1.0 copy-start.17
  191.9 513.6 %all-gather.5.cloned.1.call-start = ((), (), s32[]{:S(2)}) async-start(), calls=%async_computation.2 | async-start | bytes 7077888 | tf_op jit(solution)/shard_map/all_gather | solution.py:10
  240.1 15.6 %copy-start.2 = (bf16[2,16,128,6,64]{2,4,3,1,0:T(8,128)(2,1)S(1)}, bf16[2,16,128,6,64]{2,4,3,1,0:T(8,128)(2,1)}, u32[]{:S(2)}) copy-start(bf16[2,16,128,6,64]{2,4,3,1,0:T(8,128)(2,1)} %get-tuple-element.1665) | copy-start | bytes 9437188 | tf_op jit(solution)/shard_map/while
  240.1 15.6 %copy-start.8 = (bf16[2,16,6,64,16]{3,4,2,1,0:T(8,128)(2,1)S(1)}, bf16[2,16,6,64,16]{3,4,2,1,0:T(8,128)(2,1)}, u32[]{:S(2)}) copy-start(bf16[2,16,6,64,16]{3,4,2,1,0:T(8,128)(2,1)} %get-tuple-element.1650) | copy-start | bytes 1179652 | tf_op jit(solution)/shard_map/while
  240.1 15.6 %copy-start.11 = (bf16[2,16,128,16]{2,3,1,0:T(8,128)(2,1)S(1)}, bf16[2,16,128,16]{2,3,1,0:T(8,128)(2,1)}, u32[]{:S(2)}) copy-start(bf16[2,16,128,16]{2,3,1,0:T(8,128)(2,1)} %get-tuple-element.1668) | copy-start | bytes 393220 | tf_op jit(solution)/shard_map/while
  259.6 0.9 copy-start.9
  268.0 15.6 %copy-start.2 = (bf16[2,16,128,6,64]{2,4,3,1,0:T(8,128)(2,1)S(1)}, bf16[2,16,128,6,64]{2,4,3,1,0:T(8,128)(2,1)}, u32[]{:S(2)}) copy-start(bf16[2,16,128,6,64]{2,4,3,1,0:T(8,128)(2,1)} %get-tuple-element.1665) | copy-start | bytes 9437188 | tf_op jit(solution)/shard_map/while
  268.0 15.6 %copy-start.8 = (bf16[2,16,6,64,16]{3,4,2,1,0:T(8,128)(2,1)S(1)}, bf16[2,16,6,64,16]{3,4,2,1,0:T(8,128)(2,1)}, u32[]{:S(2)}) copy-start(bf16[2,16,6,64,16]{3,4,2,1,0:T(8,128)(2,1)} %get-tuple-element.1650) | copy-start | bytes 1179652 | tf_op jit(solution)/shard_map/while
  268.1 15.6 %copy-start.11 = (bf16[2,16,128,16]{2,3,1,0:T(8,128)(2,1)S(1)}, bf16[2,16,128,16]{2,3,1,0:T(8,128)(2,1)}, u32[]{:S(2)}) copy-start(bf16[2,16,128,16]{2,3,1,0:T(8,128)(2,1)} %get-tuple-element.1668) | copy-start | bytes 393220 | tf_op jit(solution)/shard_map/while
  287.5 0.9 copy-start.9
  289.2 6.2 copy-start.19
  289.2 458.1 %all-gather.11.cloned.1.call-start = ((), (), s32[]{:S(2)}) async-start(), calls=%async_computation.5 | async-start | bytes 7864320 | tf_op jit(solution)/shard_map/all_gather | solution.py:10
  444.6 378.9 %all-gather.9.cloned.1.call-start = ((), (), s32[]{:S(2)}) async-start(), calls=%async_computation.4 | async-start | bytes 7864320 | tf_op jit(solution)/shard_map/all_gather | solution.py:10
  572.2 11.6 %copy-start.18 = (f32[2,16,6,128]{3,1,0,2:T(8,128)S(1)}, f32[2,16,6,128]{3,1,0,2:T(8,128)}, u32[]{:S(2)}) copy-start(f32[2,16,6,128]{3,1,0,2:T(8,128)} %copy-done.17) | copy-start | bytes 294916
  870.6 6.8 copy-start.3
  870.6 6.8 copy-start.26
  877.4 12.0 %copy-start.29 = (f32[384]{0:T(512)S(1)}, f32[384]{0:T(512)}, u32[]{:S(2)}) copy-start(f32[384]{0:T(512)} %param.47) | copy-start | bytes 4612
  889.4 6.7 copy-start.30
  896.1 4.9 copy-start.28
Sparse Core Ops, SparseCore 0:
  192.0 100.2 all-gather.6
  294.5 97.2 all-gather.4
  444.7 47.6 all-gather.10
  652.3 43.8 all-gather.8
where the time goes:
time: 952 us; the launch traced here: 937 us
  matrix products  331 us (35%)
  local copies, waits for them, and re-layouts  253 us (27%)
  other arithmetic  207 us (22%)
  blocking collectives  65.2 us (7%)
  waiting for transfers between devices  45.8 us (5%)
  starting transfers between devices  18.8 us (2%)
  between operations  14 us (1%)
    dot_general x20, matrix products, block_parts(): jnp.einsum('shtu,suhp->sthp', mixing, scaled, precision=lax.Precision.HIG...  134 us
    select_n x24, other arithmetic, hop(): return jax.tree.map(lambda a, b: jnp.where(reached, a, b), new, before)  81.4 us
    dot_general x20, matrix products, block_parts(): jnp.einsum('suhp,sun->shpn', weighted, b_coef.astype(jnp.float32), precis...  65.6 us
    all_gather x4, blocking collectives, prefix(): lax.all_gather(part.astype(kind), axis)  65.2 us
    another operation x20, other arithmetic, block_parts(): cumulative = jnp.cumsum(rates, axis=2)  55.1 us
    dot_general x4, matrix products, carry_part(): jnp.einsum('stn,shpn->sthp', c_coef.astype(jnp.float32), entering, precis...  50.9 us
    all_to_all x1, waiting for transfers between devices, local(): lax.all_to_all(values, ('row', 'col'), split_axis=1, concat_axis=0, tiled...  38.8 us
    dot_general x20, matrix products, block_parts(): jnp.einsum('stn,sun->stu', c_coef, b_coef, preferred_element_type=jnp.flo...  34.1 us
  transfers between devices with their start and end apart: 10, of which 4 were waited for; matrix products, arithmetic and copies ran while one was open for 61% of the time, Pallas kernels for 0%

commit v1 on v0

v1 whole, which is shorter than its diff:
```python
import functools

import jax
import jax.numpy as jnp
from jax import lax
from jax.experimental import pallas as pl
from jax.experimental.pallas import tpu as pltpu
from jax.sharding import PartitionSpec as P

BF = jnp.bfloat16
F32 = jnp.float32
VMEM = pl.BlockSpec(memory_space=pltpu.VMEM)
PARAMS = dict(vmem_limit_bytes=56 * 1024 * 1024)
GROUP = 8
LANES = 128


def dot(a, b):
    return jnp.dot(a, b, preferred_element_type=F32)


def dot_t(a, b):
    return lax.dot_general(a, b, (((0,), (0,)), ((), ())), preferred_element_type=F32)


def silu(v):
    return v / (1.0 + jnp.exp(-v))


def rms(v, gains):
    return v * lax.rsqrt(jnp.mean(v * v, axis=-1, keepdims=True) + 1e-06) * gains


def place_kernel(cells_ref, values_ref, gain_ref, w_ref, grid_ref, x_ref, z_ref):
    tile, channels = grid_ref.shape
    slots = values_ref.shape[0]
    chunk = min(slots, 1024)
    base = pl.program_id(0) * tile
    ids = base + lax.broadcasted_iota(jnp.int32, (tile, chunk), 0)

    def add(k, acc):
        at = pl.ds(pl.multiple_of(k * chunk, chunk), chunk)
        hot = jnp.where(ids == cells_ref[:, at], 1.0, 0.0).astype(BF)
        return acc + dot(hot, values_ref[at, :])

    acc = lax.fori_loop(0, slots // chunk, add, jnp.zeros((tile, values_ref.shape[1]), F32))
    acc = acc[:, :channels]
    grid_ref[...] = acc.astype(BF)
    normed = rms(acc, gain_ref[...]).astype(BF)
    both = dot(normed, w_ref[...]).astype(BF)
    width = x_ref.shape[1]
    x_ref[...] = both[:, :width]
    z_ref[...] = both[:, width:]


def place(cells, values, gain, w, n_cells):
    channels, width = w.shape[0], w.shape[1] // 2
    tile = 512

    def whole(shape):
        return pl.BlockSpec(shape, lambda i: (0, 0))

    def rows(n):
        return pl.BlockSpec((tile, n), lambda i: (i, 0))

    return pl.pallas_call(
        place_kernel,
        grid=(n_cells // tile,),
        in_specs=[whole(cells.shape), whole(values.shape), whole(gain.shape), whole(w.shape)],
        out_specs=[rows(channels), rows(width), rows(width)],
        out_shape=[
            jax.ShapeDtypeStruct((n_cells, channels), BF),
            jax.ShapeDtypeStruct((n_cells, width), BF),
            jax.ShapeDtypeStruct((n_cells, width), BF),
        ],
        compiler_params=pltpu.CompilerParams(**PARAMS),
        name="place",
    )(cells, values, gain, w)


def lane_low(shape):
    return lax.broadcasted_iota(jnp.int32, shape, 1) < LANES // 2


def by_line(coef, lines):
    if lines == 1:
        return coef
    many = jnp.concatenate([coef] * lines, axis=0)
    line = lax.broadcasted_iota(jnp.int32, many.shape, 0) // coef.shape[0]
    own = lax.rem(lax.broadcasted_iota(jnp.int32, many.shape, 1), lines)
    return jnp.where(line == own, many, 0.0)


def coef_of(coefs, index, state):
    return coefs[index * state : (index + 1) * state, :].astype(F32)


def states(x, coefs, pair, vec, heads, state, lines, out_refs):
    for way in range(2):
        spread = by_line(coef_of(coefs, 2 * (2 * pair + way), state), lines)
        n = spread.shape[0]
        for p in range(heads // 2):
            both = jnp.concatenate(
                [spread * vec((3 + way) * heads + 2 * p + i) for i in range(2)], axis=0
            ).astype(BF)
            res = dot(both, x[:, p * LANES : (p + 1) * LANES])
            res = jnp.where(lane_low((n, LANES)), res[:n], res[n:])
            out_refs[way][:, p * LANES : (p + 1) * LANES] = res.astype(BF)


def inner(x, coefs, pair, vec, col, heads, state, lines):
    length = x.shape[0]
    shape = (length, length)
    t = lax.broadcasted_iota(jnp.int32, shape, 0)
    u = lax.broadcasted_iota(jnp.int32, shape, 1)
    ahead = t >= u
    same = t == u
    b0, c0, b1, c1 = (coefs[(4 * pair + i) * state : (4 * pair + i + 1) * state, :] for i in range(4))
    scores = jnp.where(ahead, dot_t(c0, b0), dot_t(c1, b1))
    if lines > 1:
        scores = jnp.where(lax.rem(t, lines) == lax.rem(u, lines), scores, 0.0)
    own = jnp.sum(b1.astype(F32) * c1.astype(F32), axis=0, keepdims=True)
    blocks = []
    for p in range(heads // 2):
        part = []
        for h in (2 * p, 2 * p + 1):
            gap = jnp.where(
                ahead,
                vec(h) - col[:, h : h + 1],
                vec(heads + h) - col[:, heads + h : heads + h + 1],
            )
            mix = jnp.exp(gap) * scores + jnp.where(same, vec(2 * heads + h) * own, 0.0)
            part.append(dot(mix.astype(BF), x[:, p * LANES : (p + 1) * LANES]))
        blocks.append(jnp.where(lane_low((length, LANES)), part[0], part[1]))
    return blocks


def entered(coefs, pair, vec, heads, state, lines, entering):
    spread = [by_line(coef_of(coefs, 2 * (2 * pair + way) + 1, state), lines) for way in range(2)]
    blocks = []
    for p in range(heads // 2):
        left, right = [], []
        for way in range(2):
            held = entering[way][:, p * LANES : (p + 1) * LANES].astype(F32)
            low = lane_low(held.shape)
            left += [spread[way] * vec((5 + way) * heads + 2 * p + i) for i in range(2)]
            right += [jnp.where(low, held, 0.0), jnp.where(low, 0.0, held)]
        blocks.append(
            dot_t(
                jnp.concatenate(left, axis=0).astype(BF), jnp.concatenate(right, axis=0).astype(BF)
            )
        )
    return blocks


def row_of(ref, g):
    return lambda i: ref[g, i : i + 1, :]


def conv_kernel(
    heads, state, xr_ref, left_ref, right_ref, w_ref, bias_ref, proj_ref, rv_ref, cv_ref,
    x_ref, rc_ref, cc_ref, f0_ref, f1_ref, f2_ref, f3_ref,
):
    rows_n, cols_n, width = x_ref.shape
    place = lax.broadcasted_iota(jnp.int32, (cols_n, LANES), 0)

    def one_row(r, carry):
        for b in range(width // LANES):
            at = slice(b * LANES, (b + 1) * LANES)
            tap = [0.0, 0.0, 0.0]
            edge = [0.0, 0.0]
            for i in range(3):
                v = xr_ref[r + i, :, at].astype(F32)
                for j in range(3):
                    tap[j] = tap[j] + v * w_ref[3 * i + j : 3 * i + j + 1, at]
                edge[0] = edge[0] + left_ref[r + i, :, at].astype(F32) * w_ref[3 * i : 3 * i + 1, at]
                edge[1] = (
                    edge[1] + right_ref[r + i, :, at].astype(F32) * w_ref[3 * i + 2 : 3 * i + 3, at]
                )
            total = tap[1] + bias_ref[:, at]
            total = total + jnp.where(place == 0, edge[0], pltpu.roll(tap[0], 1, 0))
            total = total + jnp.where(place == cols_n - 1, edge[1], pltpu.roll(tap[2], cols_n - 1, 0))
            x_ref[r, :, at] = silu(total).astype(BF).astype(F32)
        x = x_ref[r].astype(BF)
        coefs = lax.dot_general(
            proj_ref[...], x, (((0,), (1,)), ((), ())), preferred_element_type=F32
        ).astype(BF)
        rc_ref[r] = coefs
        states(
            x, coefs, 0, row_of(rv_ref, r), heads, state, 1, (f0_ref.at[r], f1_ref.at[r])
        )
        return carry

    lax.fori_loop(0, rows_n, one_row, 0)

    def one_group(g, carry):
        x = x_ref[:, pl.ds(pl.multiple_of(g * GROUP, GROUP), GROUP), :]
        x = x.reshape(rows_n * GROUP, width).astype(BF)
        coefs = lax.dot_general(
            proj_ref[...], x, (((0,), (1,)), ((), ())), preferred_element_type=F32
        ).astype(BF)
        cc_ref[g] = coefs
        states(
            x, coefs, 1, row_of(cv_ref, g), heads, state, GROUP, (f2_ref.at[g], f3_ref.at[g])
        )
        return carry

    lax.fori_loop(0, cols_n // GROUP, one_group, 0)


def hop(chain, axis, reverse, k, final_ref, decay_ref, enter_ref, land_ref, send_ref, send_sem, recv_sem):
    count, index = lax.axis_size(axis), lax.axis_index(axis)
    first, last = (count - 1, 0) if reverse else (0, count - 1)
    towards = index - 1 if reverse else index + 1
    lines = final_ref.shape[0]
    each = decay_ref.shape[1]
    state = final_ref.shape[1] // each

    def copy():
        return pltpu.make_async_remote_copy(
            src_ref=send_ref,
            dst_ref=land_ref,
            send_sem=send_sem.at[k],
            recv_sem=recv_sem.at[k],
            device_id={axis: towards},
            device_id_type=pl.DeviceIdType.MESH,
        )

    if chain == "send_done":

        @pl.when(index != last)
        def _():
            copy().wait_send()

        return

    @pl.when(index == first)
    def _():
        def put(i, carry):
            enter_ref[i] = jnp.zeros(enter_ref.shape[1:], BF)
            send_ref[i] = final_ref[i]
            return carry

        lax.fori_loop(0, lines, put, 0)

    @pl.when(index != first)
    def _():
        copy().wait_recv()

        def put(i, carry):
            got = land_ref[i]
            enter_ref[i] = got
            for c in range(each):
                at = slice(c * state, (c + 1) * state)
                passed = decay_ref[i, c : c + 1, :] * got[at].astype(F32) + final_ref[i, at, :].astype(F32)
                send_ref[i, at, :] = passed.astype(BF)
            return carry

        lax.fori_loop(0, lines, put, 0)

    @pl.when(index != last)
    def _():
        copy().start()


def greet(axes):
    barrier = pltpu.get_barrier_semaphore()
    peers = 0
    for axis in axes:
        count, index = lax.axis_size(axis), lax.axis_index(axis)
        for there, step in ((index > 0, -1), (index < count - 1, 1)):

            @pl.when(there)
            def _(axis=axis, step=step, index=index):
                pl.semaphore_signal(
                    barrier,
                    inc=1,
                    device_id={axis: index + step},
                    device_id_type=pl.DeviceIdType.MESH,
                )

            peers = peers + jnp.where(there, 1, 0)
    pl.semaphore_wait(barrier, peers)


def inner_kernel(heads, state, *refs):
    x_ref, rc_ref, cc_ref, rv_ref, cv_ref, ra_ref, ca_ref, skip_ref = refs[:8]
    finals, decays, (y_ref,), enters = refs[8:12], refs[12:16], refs[16:17], refs[17:21]
    lands, sends, (send_sem, recv_sem) = refs[21:25], refs[25:29], refs[29:]
    rows_n, cols_n, width = x_ref.shape
    steps = rows_n + cols_n // GROUP
    ways = (("col", False), ("col", True), ("row", False), ("row", True))

    def pass_on(what, k):
        axis, reverse = ways[k]
        hop(
            what, axis, reverse, k, finals[k], decays[k], enters[k], lands[k], sends[k], send_sem, recv_sem
        )

    def slot(k):
        axis, reverse = ways[k]
        count, index = lax.axis_size(axis), lax.axis_index(axis)
        turn = count - 1 - index if reverse else index
        if axis == "col":
            return turn * max(1, min(6, (steps - 2) // max(1, count - 1)))
        far = max(1, min(24, (steps - 8) // max(1, count // 2 - 1)))
        return turn // 2 * far + turn % 2 * min(6, far)

    greet(("row", "col"))

    def one_row(r):
        x = x_ref[r]
        blocks = inner(x.astype(BF), rc_ref[r], 0, row_of(rv_ref, r), ra_ref[r], heads, state, 1)
        for p, block in enumerate(blocks):
            at = slice(p * LANES, (p + 1) * LANES)
            y_ref[r, :, at] = block + skip_ref[:, at] * x[:, at]

    def one_group(g):
        here = pl.ds(pl.multiple_of(g * GROUP, GROUP), GROUP)
        x = x_ref[:, here, :].reshape(rows_n * GROUP, width).astype(BF)
        blocks = inner(x, cc_ref[g], 1, row_of(cv_ref, g), ca_ref[g], heads, state, GROUP)
        for p, block in enumerate(blocks):
            at = slice(p * LANES, (p + 1) * LANES)
            y_ref[:, here, at] += block.reshape(rows_n, GROUP, LANES)

    def step(s, carry):
        for k in (2, 3, 0, 1):

            @pl.when(s == slot(k))
            def _(k=k):
                pass_on("hop", k)

        @pl.when(s < rows_n)
        def _():
            one_row(s)

        @pl.when(s >= rows_n)
        def _():
            one_group(s - rows_n)

        return carry

    lax.fori_loop(0, steps, step, 0)
    for k in range(4):
        pass_on("send_done", k)


def finish_kernel(
    heads, state, y_ref, rc_ref, cc_ref, rv_ref, cv_ref, e0_ref, e1_ref, e2_ref, e3_ref,
    z_ref, grid_ref, gain_ref, out_w_ref, mlp_gain_ref, ff_in_ref, ff_out_ref, out_ref, sum_ref,
):
    rows_n, cols_n, width = y_ref.shape
    channels = out_ref.shape[2]
    span = 4

    def one_group(g, carry):
        here = pl.ds(pl.multiple_of(g * GROUP, GROUP), GROUP)
        blocks = entered(
            cc_ref[g], 1, row_of(cv_ref, g), heads, state, GROUP, (e2_ref[g], e3_ref[g])
        )
        for p, block in enumerate(blocks):
            at = slice(p * LANES, (p + 1) * LANES)
            sum_ref[:, here, at] = y_ref[:, here, at] + block.reshape(rows_n, GROUP, LANES)
        return carry

    lax.fori_loop(0, cols_n // GROUP, one_group, 0)

    def some_rows(s, carry):
        for i in range(span):
            r = s * span + i
            blocks = entered(rc_ref[r], 0, row_of(rv_ref, r), heads, state, 1, (e0_ref[r], e1_ref[r]))
            for p, block in enumerate(blocks):
                at = slice(p * LANES, (p + 1) * LANES)
                sum_ref[r, :, at] += block
        here = pl.ds(s * span, span)
        cells = span * cols_n
        total = sum_ref[here].reshape(cells, width)
        gate = z_ref[here].reshape(cells, width).astype(F32)
        gated = (rms(total, gain_ref[...]) * silu(gate)).astype(BF)
        held = grid_ref[here].reshape(cells, channels).astype(F32)
        middle = (dot(gated, out_w_ref[...]) + held).astype(BF).astype(F32)
        normed = rms(middle, mlp_gain_ref[...]).astype(BF)
        v = dot(normed, ff_in_ref[...])
        hidden = (v * 0.5 * (1.0 + lax.erf(v * 0.7071067811865476))).astype(BF)
        out = dot(hidden, ff_out_ref[...]) + middle
        out_ref[here] = out.astype(BF).reshape(span, cols_n, channels)
        return carry

    lax.fori_loop(0, rows_n // span, some_rows, 0)


def call(kernel, name, args, out_shape, scratch=(), **params):
    return pl.pallas_call(
        kernel,
        in_specs=[VMEM] * len(args),
        out_specs=[VMEM] * len(out_shape),
        out_shape=out_shape,
        scratch_shapes=list(scratch),
        compiler_params=pltpu.CompilerParams(**PARAMS, **params),
        name=name,
    )(*args)


def rate_vectors(rates, lines, per_head):
    sets, _, heads, length = rates.shape
    i = jnp.arange(length)
    own = (i[:, None] - i[None, :]) % lines == 0
    up = own & (i[:, None] <= i[None, :])
    tri = jnp.stack([up, up.T]).astype(F32)
    high = lax.Precision.HIGHEST
    cum = jnp.einsum("gkht,ktu->gkhu", rates, tri, precision=high)
    ends = jnp.einsum("gkht,tu->gkhu", rates, own.astype(F32), precision=high)
    square = -jnp.expm1(-2.0 * rates)
    weight = jnp.sqrt(square)
    shifted = cum + 0.5 * jnp.log(square)
    to_end = jnp.exp(jnp.minimum(cum - ends, 0.0)) * weight
    from_start = jnp.exp(-cum)
    both = (sets, 2 * heads, length)
    vecs = jnp.concatenate(
        [shifted.reshape(both), weight[:, 1], to_end.reshape(both), from_start.reshape(both)], axis=1
    )
    spread = jnp.repeat(jnp.eye(heads, dtype=F32), per_head, axis=1)
    decay = jnp.einsum("gkhc,hp->kgcp", jnp.exp(-ends[..., :lines]), spread, precision=high)
    return vecs, jnp.swapaxes(cum.reshape(both), 1, 2), decay


def halo(block, axis, dim):
    count = lax.axis_size(axis)
    forward = [(i, i + 1) for i in range(count - 1)]
    backward = [(b, a) for a, b in forward]
    n = block.shape[dim]
    low = lax.ppermute(lax.slice_in_dim(block, n - 1, n, axis=dim), axis, forward)
    high = lax.ppermute(lax.slice_in_dim(block, 0, 1, axis=dim), axis, backward)
    return low, high


def local(
    tile_feats, tile_cell, tile_mask, tile_count, background, norm_gain, in_x, in_z, conv_w,
    conv_bias, x_proj, skip_gain, decay_rate, out_gain, out_w, mlp_gain, ff_in, ff_out,
):
    heads, rows_n, cols_n = decay_rate.shape[1:]
    channels = tile_feats.shape[3]
    slots = tile_feats.shape[2]
    width = in_x.shape[1]
    state = x_proj.shape[1] // 8
    groups = cols_n // GROUP
    cells = rows_n * cols_n

    values = jnp.where(tile_mask[..., None] == 1, tile_feats, background)
    live = jnp.arange(slots, dtype=jnp.int32)[None, None, :] < tile_count[:, :, None]
    marked = jnp.where(live, tile_cell, cells)
    named = jnp.stack([marked // LANES, marked % LANES], axis=-1).astype(BF)
    sent = jnp.concatenate([values, named], axis=-1)
    got = lax.all_to_all(sent, ("row", "col"), split_axis=1, concat_axis=0, tiled=True)

    per_head = width // heads
    rows_first = jnp.transpose(decay_rate[:2], (2, 0, 1, 3))
    rv, ra, rd = rate_vectors(rows_first, 1, per_head)
    cols_first = jnp.transpose(
        decay_rate[2:].reshape(2, heads, rows_n, groups, GROUP), (3, 0, 1, 2, 4)
    ).reshape(groups, 2, heads, rows_n * GROUP)
    cv, ca, cd = rate_vectors(cols_first, GROUP, per_head)
    got, rv, ra, rd, cv, ca, cd = lax.optimization_barrier((got, rv, ra, rd, cv, ca, cd))

    got = got.reshape(-1, channels + 2)
    got_cells = got[:, channels:].astype(jnp.int32)
    got_cells = got_cells[:, 0] * LANES + got_cells[:, 1]
    grid, inner_x, gate = place(
        got_cells.reshape(1, -1),
        got,
        norm_gain[None],
        jnp.concatenate([in_x, in_z], axis=1),
        cells,
    )
    grid = grid.reshape(rows_n, cols_n, channels)
    gate = gate.reshape(rows_n, cols_n, width)
    inner_x = inner_x.reshape(rows_n, cols_n, width)
    top, bottom = halo(inner_x, "row", 0)
    tall = jnp.concatenate([top, inner_x, bottom], axis=0)
    left, right = halo(tall, "col", 1)

    one_row = jax.ShapeDtypeStruct((rows_n, state, width), BF)
    one_col = jax.ShapeDtypeStruct((groups, GROUP * state, width), BF)
    x, rc, cc, f0, f1, f2, f3 = call(
        functools.partial(conv_kernel, heads, state),
        "conv_states",
        (tall, left, right, conv_w.reshape(9, width), conv_bias[None], x_proj, rv, cv),
        [
            jax.ShapeDtypeStruct((rows_n, cols_n, width), F32),
            jax.ShapeDtypeStruct((rows_n, x_proj.shape[1], cols_n), BF),
            jax.ShapeDtypeStruct((groups, x_proj.shape[1], rows_n * GROUP), BF),
            one_row, one_row, one_col, one_col,
        ],
    )

    passed = [one_row, one_row, one_col, one_col]
    slots_of = [pltpu.VMEM(shape.shape, shape.dtype) for shape in passed]
    y, e0, e1, e2, e3 = call(
        functools.partial(inner_kernel, heads, state),
        "inner",
        (x, rc, cc, rv, cv, ra, ca, skip_gain[None], f0, f1, f2, f3, rd[0], rd[1], cd[0], cd[1]),
        [jax.ShapeDtypeStruct((rows_n, cols_n, width), F32)] + passed,
        scratch=slots_of + slots_of + [pltpu.SemaphoreType.DMA((4,)), pltpu.SemaphoreType.DMA((4,))],
        collective_id=0,
        has_side_effects=True,
    )
    return call(
        functools.partial(finish_kernel, heads, state),
        "finish",
        (
            y, rc, cc, rv, cv, e0, e1, e2, e3, gate, grid, out_gain[None], out_w,
            mlp_gain[None], ff_in, ff_out,
        ),
        [jax.ShapeDtypeStruct((rows_n, cols_n, channels), BF)],
        scratch=[pltpu.VMEM((rows_n, cols_n, width), F32)],
    )[0]


def solution(mesh):
    placed = (
        P(("row", "col"), None, None, None),
        P(("row", "col"), None, None),
        P(("row", "col"), None, None),
        P(("row", "col"), None),
        P(), P(), P(), P(), P(), P(), P(), P(),
        P(None, None, "row", "col"),
        P(), P(), P(), P(), P(),
    )
    return jax.shard_map(
        local, mesh=mesh, in_specs=placed, out_specs=P("row", "col", None), check_vma=False
    )
```

time: 952 us -> 251 us (0.26); the launches traced: 937 us -> 250 us
  matrix products: 331 us -> 4.71 us
  local copies, waits for them, and re-layouts: 253 us -> 38.4 us
  other arithmetic: 207 us -> 16.4 us
  Pallas kernels: 0 us -> 168 us
  blocking collectives: 65.2 us -> 0 us
  waiting for transfers between devices: 45.8 us -> 6.71 us
  between operations: 14 us -> 0.33 us
    dot_general x69 -> x6, matrix products: 331 us -> 4.71 us  [the longest x2 1.59 us: rate_vectors(): ends = jnp.einsum('gkht,tu->gkhu', rates, own.astype(F32), precision=high)]
    pallas_call x0 -> x4, Pallas kernels: none -> 168 us  [the longest x3 146 us: call(): pl.pallas_call(kernel, in_specs=[VMEM] * len(args), out_specs=[VMEM] * le...]
    select_n x26 -> x0, other arithmetic: 82.9 us -> none  [the longest x24 81.4 us: hop(): return jax.tree.map(lambda a, b: jnp.where(reached, a, b), new, before)]
    rev x15 -> x0, local copies, waits for them, and re-layouts: 66.7 us -> none  [the longest x2 27.5 us: restore(): result = jnp.flip(result, 1)]
    all_gather x4 -> x0, blocking collectives: 65.2 us -> none  [prefix(): lax.all_gather(part.astype(kind), axis)]
    another operation x20 -> x1, other arithmetic: 55.1 us -> 0.81 us  [local(): named = jnp.stack([marked // LANES, marked % LANES], axis=-1).astype(BF)]
    transpose x30 -> x2, local copies, waits for them, and re-layouts: 43.6 us -> 1.75 us  [the longest x1 1.68 us: local(): jnp.transpose(decay_rate[2:].reshape(2, heads, rows_n, groups, GROUP), (3...]
    all_to_all x2 -> x1, waiting for transfers between devices: 42.4 us -> 1.07 us  [local(): lax.all_to_all(sent, ('row', 'col'), split_axis=1, concat_axis=0, tiled=T...]
  transfers between devices with their start and end apart: 10 -> 5, of which waited for: 4 -> 3; matrix products, arithmetic and copies ran while one was open for 61% -> 16% of each run, Pallas kernels for 0% -> 0%
where the time goes in v1:
time: 251 us; the launch traced here: 250 us
  Pallas kernels  168 us (67%)
  local copies, waits for them, and re-layouts  38.4 us (15%)
  other arithmetic  16.4 us (7%)
  starting transfers between devices  15 us (6%)
  waiting for transfers between devices  6.71 us (3%)
  matrix products  4.71 us (2%)
    pallas_call x3, Pallas kernels, call(): pl.pallas_call(kernel, in_specs=[VMEM] * len(args), out_specs=[VMEM] * le...  146 us
    pallas_call x1, Pallas kernels, place(): pl.pallas_call(place_kernel, grid=(n_cells // tile,), in_specs=[whole(cel...  21.9 us
    all_to_all x1, starting transfers between devices, local(): lax.all_to_all(sent, ('row', 'col'), split_axis=1, concat_axis=0, tiled=T...  7.3 us
    unnamed x41, local copies, waits for them, and re-layouts  5.73 us
    ppermute x2, waiting for transfers between devices, halo(): high = lax.ppermute(lax.slice_in_dim(block, 0, 1, axis=dim), axis, backward)  5.64 us
  transfers between devices with their start and end apart: 5, of which 3 were waited for; matrix products, arithmetic and copies ran while one was open for 16% of the time, Pallas kernels for 0%

profile of v1, /device:TPU:0, one launch (start us, length us, event | category | flops | bytes accessed | tf_op | source)
XLA Modules:
  0.0 249.5 jit_solution(2902087170794465606)
XLA Ops:
  0.0 0.8 fusion.58
  0.9 0.7 compare_bitcast_fusion
  1.6 1.6 bitcast_select_fusion
  3.2 1.3 pad_maximum_fusion.1
  4.5 7.3 %all-to-all-start = ((bf16[1,32,128,194]{2,3,0,1:T(8,128)(2,1)}), bf16[1,32,128,194]{2,3,0,1:T(8,128)(2,1)S(1)}, u32[]{:S(2)}, u32[]{:S(2)}) async-start(bf16[1,32,128,194]{2,3,0,1:T(8,128)(2,1)} %pad_maximum_fusion.1), calls=%async_computation | async-start | bytes 3276800 | tf_op jit(solution)/shard_map/all_to_all | solution.py:454
  11.8 0.2 fusion.31
  12.1 0.7 fusion.71
  12.8 1.2 copy.204
  13.9 1.7 copy.174
  15.6 1.4 fusion.34
  17.0 0.7 broadcast_in_dim.51
  17.7 1.4 reshape.382
  19.1 1.4 reshape.379
  20.5 1.3 copy.177
  21.8 0.8 copy.249
  22.6 1.4 fusion.1
  24.0 2.1 bitcast_add_fusion
  26.1 0.1 copy.184
  26.3 0.8 copy.185
  27.2 0.8 copy.186
  28.0 0.2 fusion.40
  28.2 0.1 copy.250
  28.4 0.2 fusion.38
  28.6 1.2 bitcast_add_fusion.1
  29.9 0.8 copy.166
  30.8 0.8 copy.167
  31.6 0.8 copy.168
  32.4 2.0 copy.188
  34.4 2.0 copy.170
  36.5 0.2 copy.171
  36.6 0.6 reshape.374.w_ref
  37.2 1.3 broadcast_in_dim.53.bias_ref
  38.6 1.2 broadcast_in_dim.54.refs_7_
  39.8 1.9 copy.192.ff_out_ref
  41.7 0.8 copy.191.out_w_ref
  42.5 1.2 broadcast_in_dim.55.gain_ref
  43.7 1.0 fusion.56
  44.8 1.7 pad_maximum_fusion.4.w_ref
  46.5 1.0 slice_bitcast_fusion.2
  47.5 1.0 pad_maximum_fusion.3.cv_ref.refs_4_
  48.5 0.9 slice_bitcast_fusion.3
  49.5 1.0 pad_maximum_fusion.2.rv_ref.refs_3_
  50.5 0.5 convolution_bitcast_fusion
  51.0 1.1 all-to-all-done
  52.1 1.2 copy-done.2
  53.3 3.2 %copy.190 = bf16[32,1,128,194]{3,2,0,1:T(8,128)(2,1)S(1)} copy(bf16[32,1,128,194]{2,3,0,1:T(8,128)(2,1)} %bitcast.137) | data formatting | bytes 3178496 | tf_op jit(solution)/shard_map/optimization_barrier | solution.py:463
  56.5 0.5 slice_convert_fusion
  57.0 1.8 fusion
  58.7 21.9 %place.1 = (bf16[4096,192]{1,0:T(8,128)(2,1)}, bf16[4096,384]{1,0:T(8,128)(2,1)}, bf16[4096,384]{1,0:T(8,128)(2,1)}) custom-call(s32[1,4096]{1,0:T(1,128)} %bitcast.152, bf16[4096,194]{1,0:T(8,128)(2,1)} %bitcast.134, f32[1,192]{1,0:T(1,128)} %bitcast.154, bf16[192,768]{1,0:T(8,128)(2,1)} %pad_maximum_fusion.4.w_ref), custom_call_target="tpu_custom_call" | custom-call | tf_op jit(solution)/shard_map/place/pallas_call | solution.py:66
  80.7 1.0 slice_bitcast_fusion.5
  81.6 1.6 collective-permute-start
  83.2 1.5 collective-permute-start.1
  84.7 0.8 slice_bitcast_fusion
  85.5 1.6 collective-permute-done.1
  87.1 2.4 pad_maximum_fusion.xr_ref
  89.6 3.4 %collective-permute-start.2 = (bf16[34,1,384]{2,1,0:T(2,128)(2,1)S(1)}, bf16[34,1,384]{2,1,0:T(2,128)(2,1)S(1)}, u32[]{:S(2)}, u32[]{:S(2)}) collective-permute-start(bf16[34,1,384]{2,1,0:T(2,128)(2,1)S(1)} %get-tuple-element.50), channel_id=1, source_target_pairs={{0,1},{1,2},{2,3},{3,4},{4,5},{5,6},{6,7},{8,9},{9,10},{10,11},{11... | collective-permute-start | bytes 78344 | tf_op jit(solution)/shard_map/ppermute | solution.py:432
  93.0 1.3 collective-permute-start.3
  94.3 0.7 slice_bitcast_fusion.6
  94.9 4.0 %collective-permute-done.3.right_ref = bf16[34,1,384]{2,1,0:T(2,128)(2,1)S(1)} collective-permute-done((bf16[34,1,384]{2,1,0:T(2,128)(2,1)S(1)}, bf16[34,1,384]{2,1,0:T(2,128)(2,1)S(1)}, u32[]{:S(2)}, u32[]{:S(2)}) %collective-permute-start.3) | collective-permute-done | bytes 26144 | tf_op jit(solution)/shard_map/ppermute | solution.py:433
  99.0 0.6 copy-done.16
  99.6 33.7 %conv_states.1 = (f32[32,128,384]{2,1,0:T(8,128)}, bf16[32,128,128]{2,1,0:T(8,128)(2,1)}, bf16[16,128,256]{2,1,0:T(8,128)(2,1)}, bf16[32,16,384]{2,1,0:T(8,128)(...) custom-call(bf16[34,128,384]{2,1,0:T(8,128)(2,1)} %copy-done, ...), custom_call_target="tpu_custom_call" | custom-call | tf_op jit(solution)/shard_map/conv_states/pallas_call | solution.py:393
  133.3 86.4 %inner.1 = (f32[32,128,384]{2,1,0:T(8,128)}, bf16[32,16,384]{2,1,0:T(8,128)(2,1)}, bf16[32,16,384]{2,1,0:T(8,128)(2,1)}, bf16[16,128,384]{2,1,0:T(8,128)(2,1)}, bf16[16,128,384]{2,1,0:T(8,128)(2,1)}) custom-call(f32[32,128,384]{2,1,0:T(8,128)} %get-tuple-element.31.refs_0_, bf16[32,128,128]{2,1,0:T(8,128)(2,1)} %get-tuple-element.32.refs_1_.rc_ref, ...), custom_call_target="tpu_custom_call" | custom-call | tf_op jit(solution)/shard_map/inner/pallas_call | solution.py:393
  219.7 25.9 %finish.1 = bf16[32,128,192]{2,1,0:T(8,128)(2,1)} custom-call(f32[32,128,384]{2,1,0:T(8,128)} %get-tuple-element.42.y_ref, bf16[32,128,128]{2,1,0:T(8,128)(2,1)} %get-tuple-element.32.refs_1_.rc_ref, bf16[16,128,256]{2,1,0:T(8,128)(2,1)} %get-tuple-element.33.refs_2_.cc_ref, f32[32,42,128]{2,1,0:T(8,128)} %pad_maximum_fusion.2.rv_ref.refs_3_, ...), custom_call_target="tpu_custom_call" | custom-call | tf_op jit(solution)/shard_map/finish/pallas_call | solution.py:393
  245.6 3.9 %copy.193 = bf16[32,128,192]{1,2,0:T(8,128)(2,1)} copy(bf16[32,128,192]{2,1,0:T(8,128)(2,1)} %finish.1) | data formatting | bytes 3145728 | tf_op jit(solution)/shard_map/finish/pallas_call | solution.py:393
  (51 shorter events, 0.6 us)
Async XLA Ops:
  4.5 7.5 %copy-start.4 = (f32[4,6,32,128]{3,2,1,0:T(8,128)S(1)}, f32[4,6,32,128]{3,2,1,0:T(8,128)}, u32[]{:S(2)}) copy-start(f32[4,6,32,128]{3,2,1,0:T(8,128)} %param.30) | copy-start | bytes 1179652
  4.5 47.6 %all-to-all-start = ((bf16[1,32,128,194]{2,3,0,1:T(8,128)(2,1)}), bf16[1,32,128,194]{2,3,0,1:T(8,128)(2,1)S(1)}, u32[]{:S(2)}, u32[]{:S(2)}) async-start(bf16[1,32,128,194]{2,3,0,1:T(8,128)(2,1)} %pad_maximum_fusion.1), calls=%async_computation | async-start | bytes 3276800 | tf_op jit(solution)/shard_map/all_to_all | solution.py:454
  17.0 5.6 %copy-start.3 = (f32[256,16,2,6]{0,1,3,2:T(8,128)}, f32[256,16,2,6]{0,1,3,2:T(8,128)S(1)}, u32[]{:S(2)}) copy-start(f32[256,16,2,6]{0,1,3,2:T(8,128)S(1)} %fusion.34) | copy-start | bytes 589828
  21.8 2.2 copy-start.6
  24.0 4.0 %copy-start.5 = (f32[4,6,32,128]{3,2,1,0:T(8,128)S(1)}, f32[4,6,32,128]{3,2,1,0:T(8,128)}, u32[]{:S(2)}) copy-start(f32[4,6,32,128]{3,2,1,0:T(8,128)} %param.30) | copy-start | bytes 1179652
  26.0 2.6 %copy-start.12 = (f32[2,6,32,128]{3,2,1,0:T(8,128)S(1)}, f32[2,6,32,128]{3,2,1,0:T(8,128)}, u32[]{:S(2)}) copy-start(f32[2,6,32,128]{3,2,1,0:T(8,128)} %get-tuple-element.58) | copy-start | bytes 589828
  34.4 2.2 copy-start.18
  34.4 7.3 %copy-start.14 = (bf16[384,192]{0,1:T(8,128)(2,1)S(1)}, bf16[384,192]{0,1:T(8,128)(2,1)}, u32[]{:S(2)}) copy-start(bf16[384,192]{0,1:T(8,128)(2,1)} %param.32) | copy-start | bytes 442372
  36.4 11.1 %copy-start.7 = (f32[16,12,256]{2,1,0:T(8,128)S(1)}, f32[16,12,256]{2,1,0:T(8,128)}, u32[]{:S(2)}) copy-start(f32[16,12,256]{2,1,0:T(8,128)} %copy.185) | copy-start | bytes 589828
  36.4 11.1 %copy-start.8 = (f32[16,12,256]{2,1,0:T(8,128)S(1)}, f32[16,12,256]{2,1,0:T(8,128)}, u32[]{:S(2)}) copy-start(f32[16,12,256]{2,1,0:T(8,128)} %copy.186) | copy-start | bytes 589828
  37.2 12.2 %copy-start.9 = (f32[32,12,128]{2,1,0:T(8,128)S(1)}, f32[32,12,128]{2,1,0:T(8,128)}, u32[]{:S(2)}) copy-start(f32[32,12,128]{2,1,0:T(8,128)} %copy.166) | copy-start | bytes 589828
  37.2 12.2 %copy-start.10 = (f32[32,12,128]{2,1,0:T(8,128)S(1)}, f32[32,12,128]{2,1,0:T(8,128)}, u32[]{:S(2)}) copy-start(f32[32,12,128]{2,1,0:T(8,128)} %copy.167) | copy-start | bytes 589828
  37.2 12.2 %copy-start.11 = (f32[32,12,128]{2,1,0:T(8,128)S(1)}, f32[32,12,128]{2,1,0:T(8,128)}, u32[]{:S(2)}) copy-start(f32[32,12,128]{2,1,0:T(8,128)} %copy.168) | copy-start | bytes 589828
  46.5 4.0 %copy-start.13 = (f32[256,16,2,6]{0,3,1,2:T(8,128)S(1)}, f32[256,16,2,6]{0,3,1,2:T(8,128)}, u32[]{:S(2)}) copy-start(f32[256,16,2,6]{0,3,1,2:T(8,128)} %copy.249) | copy-start | bytes 589828
  46.5 4.0 %copy-start.17 = (f32[6,384,1,1]{1,0,2,3:T(8,128)S(1)}, f32[6,384,1,1]{1,0,2,3:T(8,128)}, u32[]{:S(2)}) copy-start(f32[6,384,1,1]{1,0,2,3:T(8,128)} %reshape.382) | copy-start | bytes 27652
  52.1 1.2 copy-start.2
  56.5 2.3 copy-start.1
  81.6 3.8 %collective-permute-start = (bf16[1,128,384]{2,1,0:T(8,128)(2,1)S(1)}, bf16[1,128,384]{2,1,0:T(8,128)(2,1)S(1)}, u32[]{:S(2)}, u32[]{:S(2)}) collective-permute-start(bf16[1,128,384]{2,1,0:T(8,128)(2,1)S(1)} %get-tuple-element.51), channel_id=1, source_target_pairs={{0,8},{8,16},{16,24},{1,9},{9,17},{17,25},{2,10},{10,18},{18,26},{... | collective-permute-start | bytes 294920 | tf_op jit(solution)/shard_map/ppermute | solution.py:432
  83.2 3.9 %collective-permute-start.1 = (bf16[1,128,384]{2,1,0:T(8,128)(2,1)S(1)}, bf16[1,128,384]{2,1,0:T(8,128)(2,1)S(1)}, u32[]{:S(2)}, u32[]{:S(2)}) collective-permute-start(bf16[1,128,384]{2,1,0:T(8,128)(2,1)S(1)} %get-tuple-element.52), channel_id=1, source_target_pairs={{8,0},{16,8},{24,16},{9,1},{17,9},{25,17},{10,2},{18,10},{26,18},{... | collective-permute-start | bytes 294920 | tf_op jit(solution)/shard_map/ppermute | solution.py:433
  89.5 9.5 %copy-start = (bf16[34,128,384]{2,1,0:T(8,128)(2,1)}, bf16[34,128,384]{2,1,0:T(8,128)(2,1)S(1)}, u32[]{:S(2)}) copy-start(bf16[34,128,384]{2,1,0:T(8,128)(2,1)S(1)} %pad_maximum_fusion.xr_ref) | copy-start | bytes 10027012
  89.6 5.4 %collective-permute-start.2 = (bf16[34,1,384]{2,1,0:T(2,128)(2,1)S(1)}, bf16[34,1,384]{2,1,0:T(2,128)(2,1)S(1)}, u32[]{:S(2)}, u32[]{:S(2)}) collective-permute-start(bf16[34,1,384]{2,1,0:T(2,128)(2,1)S(1)} %get-tuple-element.50), channel_id=1, source_target_pairs={{0,1},{1,2},{2,3},{3,4},{4,5},{5,6},{6,7},{8,9},{9,10},{10,11},{11... | collective-permute-start | bytes 78344 | tf_op jit(solution)/shard_map/ppermute | solution.py:432
  93.0 6.0 %collective-permute-start.3 = (bf16[34,1,384]{2,1,0:T(2,128)(2,1)S(1)}, bf16[34,1,384]{2,1,0:T(2,128)(2,1)S(1)}, u32[]{:S(2)}, u32[]{:S(2)}) collective-permute-start(bf16[34,1,384]{2,1,0:T(2,128)(2,1)S(1)} %get-tuple-element.49), channel_id=1, source_target_pairs={{1,0},{2,1},{3,2},{4,3},{5,4},{6,5},{7,6},{9,8},{10,9},{11,10},{12... | collective-permute-start | bytes 78344 | tf_op jit(solution)/shard_map/ppermute | solution.py:433
  94.9 4.0 %copy-start.15 = (bf16[34,1,384]{2,1,0:T(2,128)(2,1)}, bf16[34,1,384]{2,1,0:T(2,128)(2,1)S(1)}, u32[]{:S(2)}) copy-start(bf16[34,1,384]{2,1,0:T(2,128)(2,1)S(1)} %collective-permute-done.2.left_ref) | copy-start | bytes 78340
  99.0 0.6 copy-start.16

commit v2 on v1

--- a/solution.py
+++ b/solution.py
@@ -13,6 +13,8 @@
 PARAMS = dict(vmem_limit_bytes=56 * 1024 * 1024)
 GROUP = 8
 LANES = 128
+SPAN = 4
+PARTS = 4
 
 
 def dot(a, b):
@@ -191,7 +193,7 @@
         )
         return carry
 
-    lax.fori_loop(0, rows_n, one_row, 0)
+    lax.fori_loop(0, rows_n, one_row, 0, unroll=2)
 
     def one_group(g, carry):
         x = x_ref[:, pl.ds(pl.multiple_of(g * GROUP, GROUP), GROUP), :]
@@ -205,28 +207,31 @@
         )
         return carry
 
-    lax.fori_loop(0, cols_n // GROUP, one_group, 0)
-
-
-def hop(chain, axis, reverse, k, final_ref, decay_ref, enter_ref, land_ref, send_ref, send_sem, recv_sem):
+    lax.fori_loop(0, cols_n // GROUP, one_group, 0, unroll=2)
+
+
+def hop(what, axis, reverse, k, part, final_ref, decay_ref, enter_ref, land_ref, send_ref, sems):
     count, index = lax.axis_size(axis), lax.axis_index(axis)
     first, last = (count - 1, 0) if reverse else (0, count - 1)
     towards = index - 1 if reverse else index + 1
-    lines = final_ref.shape[0]
+    lines = final_ref.shape[0] // PARTS
+    here = pl.ds(part * lines, lines)
+    k = k * PARTS + part
+    send_sem, recv_sem = sems
     each = decay_ref.shape[1]
     state = final_ref.shape[1] // each
 
     def copy():
         return pltpu.make_async_remote_copy(
-            src_ref=send_ref,
-            dst_ref=land_ref,
+            src_ref=send_ref.at[here],
+            dst_ref=land_ref.at[here],
             send_sem=send_sem.at[k],
             recv_sem=recv_sem.at[k],
             device_id={axis: towards},
             device_id_type=pl.DeviceIdType.MESH,
         )
 
-    if chain == "send_done":
+    if what == "send_done":
 
         @pl.when(index != last)
         def _():
@@ -241,7 +246,7 @@
             send_ref[i] = final_ref[i]
             return carry
 
-        lax.fori_loop(0, lines, put, 0)
+        lax.fori_loop(part * lines, (part + 1) * lines, put, 0)
 
     @pl.when(index != first)
     def _():
@@ -256,7 +261,7 @@
                 send_ref[i, at, :] = passed.astype(BF)
             return carry
 
-        lax.fori_loop(0, lines, put, 0)
+        lax.fori_loop(part * lines, (part + 1) * lines, put, 0)
 
     @pl.when(index != last)
     def _():
@@ -286,34 +291,40 @@
 def inner_kernel(heads, state, *refs):
     x_ref, rc_ref, cc_ref, rv_ref, cv_ref, ra_ref, ca_ref, skip_ref = refs[:8]
     finals, decays, (y_ref,), enters = refs[8:12], refs[12:16], refs[16:17], refs[17:21]
-    lands, sends, (send_sem, recv_sem) = refs[21:25], refs[25:29], refs[29:]
+    lands, sends, sems = refs[21:25], refs[25:29], refs[29:]
     rows_n, cols_n, width = x_ref.shape
-    steps = rows_n + cols_n // GROUP
+    row_steps = rows_n // 2
+    steps = row_steps + cols_n // GROUP
     ways = (("col", False), ("col", True), ("row", False), ("row", True))
 
-    def pass_on(what, k):
+    def pass_on(what, k, part):
         axis, reverse = ways[k]
         hop(
-            what, axis, reverse, k, finals[k], decays[k], enters[k], lands[k], sends[k], send_sem, recv_sem
+            what, axis, reverse, k, part, finals[k], decays[k], enters[k], lands[k], sends[k], sems
         )
 
-    def slot(k):
+    def slot(k, part):
         axis, reverse = ways[k]
         count, index = lax.axis_size(axis), lax.axis_index(axis)
         turn = count - 1 - index if reverse else index
-        if axis == "col":
-            return turn * max(1, min(6, (steps - 2) // max(1, count - 1)))
-        far = max(1, min(24, (steps - 8) // max(1, count // 2 - 1)))
-        return turn // 2 * far + turn % 2 * min(6, far)
+        apart, each = (2, 3) if axis == "col" else (3, 4)
+        each = max(1, min(each, (steps - 1 - (PARTS - 1) * apart) // max(1, count - 1)))
+        return turn * each + part * apart
 
     greet(("row", "col"))
 
-    def one_row(r):
-        x = x_ref[r]
-        blocks = inner(x.astype(BF), rc_ref[r], 0, row_of(rv_ref, r), ra_ref[r], heads, state, 1)
-        for p, block in enumerate(blocks):
-            at = slice(p * LANES, (p + 1) * LANES)
-            y_ref[r, :, at] = block + skip_ref[:, at] * x[:, at]
+    def two_rows(s):
+        done = []
+        for r in (2 * s, 2 * s + 1):
+            x = x_ref[r]
+            blocks = inner(x.astype(BF), rc_ref[r], 0, row_of(rv_ref, r), ra_ref[r], heads, state, 1)
+            done.append([
+                block + skip_ref[:, p * LANES : (p + 1) * LANES] * x[:, p * LANES : (p + 1) * LANES]
+                for p, block in enumerate(blocks)
+            ])
+        for i in range(2):
+            for p, block in enumerate(done[i]):
+                y_ref[2 * s + i, :, p * LANES : (p + 1) * LANES] = block
 
     def one_group(g):
         here = pl.ds(pl.multiple_of(g * GROUP, GROUP), GROUP)
@@ -324,34 +335,40 @@
             y_ref[:, here, at] += block.reshape(rows_n, GROUP, LANES)
 
     def step(s, carry):
-        for k in (2, 3, 0, 1):
-
-            @pl.when(s == slot(k))
-            def _(k=k):
-                pass_on("hop", k)
-
-        @pl.when(s < rows_n)
+        for part in range(PARTS):
+            for k in (0, 1, 2, 3):
+
+                @pl.when(s == slot(k, part))
+                def _(k=k, part=part):
+                    pass_on("hop", k, part)
+
+        @pl.when(s < row_steps)
         def _():
-            one_row(s)
-
-        @pl.when(s >= rows_n)
+            two_rows(s)
+
+        @pl.when(s >= row_steps)
         def _():
-            one_group(s - rows_n)
+            one_group(s - row_steps)
 
         return carry
 
     lax.fori_loop(0, steps, step, 0)
     for k in range(4):
-        pass_on("send_done", k)
+        for part in range(PARTS):
+            pass_on("send_done", k, part)
 
 
 def finish_kernel(
     heads, state, y_ref, rc_ref, cc_ref, rv_ref, cv_ref, e0_ref, e1_ref, e2_ref, e3_ref,
-    z_ref, grid_ref, gain_ref, out_w_ref, mlp_gain_ref, ff_in_ref, ff_out_ref, out_ref, sum_ref,
+    z_ref, grid_ref, gain_ref, out_w_ref, mlp_gain_ref, ff_in_ref, ff_out_ref, out_ref, sum_ref, held_ref, sem,
 ):
     rows_n, cols_n, width = y_ref.shape
     channels = out_ref.shape[2]
-    span = 4
+    span = SPAN
+
+    def leave(s):
+        here = pl.ds(s * span, span)
+        return pltpu.make_async_copy(held_ref.at[here], out_ref.at[here], sem.at[s])
 
     def one_group(g, carry):
         here = pl.ds(pl.multiple_of(g * GROUP, GROUP), GROUP)
@@ -383,17 +400,24 @@
         v = dot(normed, ff_in_ref[...])
         hidden = (v * 0.5 * (1.0 + lax.erf(v * 0.7071067811865476))).astype(BF)
         out = dot(hidden, ff_out_ref[...]) + middle
-        out_ref[here] = out.astype(BF).reshape(span, cols_n, channels)
+        held_ref[here] = out.astype(BF).reshape(span, cols_n, channels)
+        leave(s).start()
         return carry
 
     lax.fori_loop(0, rows_n // span, some_rows, 0)
 
-
-def call(kernel, name, args, out_shape, scratch=(), **params):
+    def left(s, carry):
+        leave(s).wait()
+        return carry
+
+    lax.fori_loop(0, rows_n // span, left, 0)
+
+
+def call(kernel, name, args, out_shape, scratch=(), out_space=pltpu.VMEM, **params):
     return pl.pallas_call(
         kernel,
         in_specs=[VMEM] * len(args),
-        out_specs=[VMEM] * len(out_shape),
+        out_specs=[pl.BlockSpec(memory_space=out_space)] * len(out_shape),
         out_shape=out_shape,
         scratch_shapes=list(scratch),
         compiler_params=pltpu.CompilerParams(**PARAMS, **params),
@@ -500,7 +524,7 @@
         "inner",
         (x, rc, cc, rv, cv, ra, ca, skip_gain[None], f0, f1, f2, f3, rd[0], rd[1], cd[0], cd[1]),
         [jax.ShapeDtypeStruct((rows_n, cols_n, width), F32)] + passed,
-        scratch=slots_of + slots_of + [pltpu.SemaphoreType.DMA((4,)), pltpu.SemaphoreType.DMA((4,))],
+        scratch=slots_of + slots_of + [pltpu.SemaphoreType.DMA((4 * PARTS,))] * 2,
         collective_id=0,
         has_side_effects=True,
     )
@@ -512,7 +536,12 @@
             mlp_gain[None], ff_in, ff_out,
         ),
         [jax.ShapeDtypeStruct((rows_n, cols_n, channels), BF)],
-        scratch=[pltpu.VMEM((rows_n, cols_n, width), F32)],
+        scratch=[
+            pltpu.VMEM((rows_n, cols_n, width), F32),
+            pltpu.VMEM((rows_n, cols_n, channels), BF),
+            pltpu.SemaphoreType.DMA((rows_n // SPAN,)),
+        ],
+        out_space=pl.ANY,
     )[0]
 
 

time: 251 us -> 218 us (0.87)
  Pallas kernels: 168 us -> 136 us
    pallas_call x3, Pallas kernels: 146 us -> 114 us  [call(): pl.pallas_call(kernel, in_specs=[VMEM] * len(args), out_specs=[pl.BlockSp...]
  transfers between devices with their start and end apart: 5 -> 5, of which waited for: 3 -> 3; matrix products, arithmetic and copies ran while one was open for 16% -> 19% of each run, Pallas kernels for 0% -> 0%
where the time goes in v2:
time: 218 us; the launch traced here: 217 us
  Pallas kernels  136 us (62%)
  local copies, waits for them, and re-layouts  38.4 us (18%)
  other arithmetic  16.4 us (8%)
  starting transfers between devices  15 us (7%)
  waiting for transfers between devices  6.71 us (3%)
  matrix products  4.71 us (2%)
    pallas_call x3, Pallas kernels, call(): pl.pallas_call(kernel, in_specs=[VMEM] * len(args), out_specs=[pl.BlockSp...  114 us
    pallas_call x1, Pallas kernels, place(): pl.pallas_call(place_kernel, grid=(n_cells // tile,), in_specs=[whole(cel...  21.9 us
    all_to_all x1, starting transfers between devices, local(): lax.all_to_all(sent, ('row', 'col'), split_axis=1, concat_axis=0, tiled=T...  7.3 us
    unnamed x41, local copies, waits for them, and re-layouts  5.73 us
    ppermute x2, waiting for transfers between devices, halo(): high = lax.ppermute(lax.slice_in_dim(block, 0, 1, axis=dim), axis, backward)  5.64 us
    ppermute x2, starting transfers between devices, halo(): lax.ppermute(lax.slice_in_dim(block, n - 1, n, axis=dim), axis, forward)  4.94 us
  transfers between devices with their start and end apart: 5, of which 3 were waited for; matrix products, arithmetic and copies ran while one was open for 19% of the time, Pallas kernels for 0%

profile of v2, /device:TPU:0, one launch (start us, length us, event | category | flops | bytes accessed | tf_op | source)
XLA Modules:
  0.0 217.3 jit_solution(5672905102296628810)
XLA Ops:
  0.0 0.8 fusion.58
  0.9 0.7 compare_bitcast_fusion
  1.6 1.6 bitcast_select_fusion
  3.2 1.3 pad_maximum_fusion.1
  4.5 7.3 %all-to-all-start = ((bf16[1,32,128,194]{2,3,0,1:T(8,128)(2,1)}), bf16[1,32,128,194]{2,3,0,1:T(8,128)(2,1)S(1)}, u32[]{:S(2)}, u32[]{:S(2)}) async-start(bf16[1,32,128,194]{2,3,0,1:T(8,128)(2,1)} %pad_maximum_fusion.1), calls=%async_computation | async-start | bytes 3276800 | tf_op jit(solution)/shard_map/all_to_all | solution.py:478
  11.8 0.2 fusion.31
  12.1 0.7 fusion.71
  12.8 1.2 copy.204
  13.9 1.7 copy.174
  15.6 1.4 fusion.34
  17.0 0.7 broadcast_in_dim.51
  17.7 1.4 reshape.382
  19.1 1.4 reshape.379
  20.5 1.3 copy.177
  21.8 0.8 copy.249
  22.6 1.4 fusion.1
  24.0 2.1 bitcast_add_fusion
  26.1 0.1 copy.184
  26.3 0.8 copy.185
  27.2 0.8 copy.186
  28.0 0.2 fusion.40
  28.2 0.1 copy.250
  28.4 0.2 fusion.38
  28.6 1.2 bitcast_add_fusion.1
  29.9 0.8 copy.166
  30.8 0.8 copy.167
  31.6 0.8 copy.168
  32.4 2.0 copy.188
  34.4 2.0 copy.170
  36.5 0.2 copy.171
  36.6 0.6 reshape.374.w_ref
  37.2 1.3 broadcast_in_dim.53.bias_ref
  38.6 1.2 broadcast_in_dim.54.refs_7_
  39.8 1.9 copy.192.ff_out_ref
  41.7 0.8 copy.191.out_w_ref
  42.5 1.2 broadcast_in_dim.55.gain_ref
  43.7 1.0 fusion.56
  44.8 1.7 pad_maximum_fusion.4.w_ref
  46.5 1.0 slice_bitcast_fusion.2
  47.5 1.0 pad_maximum_fusion.3.cv_ref.refs_4_
  48.5 0.9 slice_bitcast_fusion.3
  49.5 1.0 pad_maximum_fusion.2.rv_ref.refs_3_
  50.5 0.5 convolution_bitcast_fusion
  51.0 1.1 all-to-all-done
  52.1 1.2 copy-done.2
  53.3 3.2 %copy.190 = bf16[32,1,128,194]{3,2,0,1:T(8,128)(2,1)S(1)} copy(bf16[32,1,128,194]{2,3,0,1:T(8,128)(2,1)} %bitcast.137) | data formatting | bytes 3178496 | tf_op jit(solution)/shard_map/optimization_barrier | solution.py:487
  56.5 0.5 slice_convert_fusion
  57.0 1.8 fusion
  58.7 21.9 %place.1 = (bf16[4096,192]{1,0:T(8,128)(2,1)}, bf16[4096,384]{1,0:T(8,128)(2,1)}, bf16[4096,384]{1,0:T(8,128)(2,1)}) custom-call(s32[1,4096]{1,0:T(1,128)} %bitcast.152, bf16[4096,194]{1,0:T(8,128)(2,1)} %bitcast.134, f32[1,192]{1,0:T(1,128)} %bitcast.154, bf16[192,768]{1,0:T(8,128)(2,1)} %pad_maximum_fusion.4.w_ref), custom_call_target="tpu_custom_call" | custom-call | tf_op jit(solution)/shard_map/place/pallas_call | solution.py:68
  80.7 1.0 slice_bitcast_fusion.5
  81.6 1.6 collective-permute-start
  83.2 1.5 collective-permute-start.1
  84.7 0.8 slice_bitcast_fusion
  85.5 1.6 collective-permute-done.1
  87.1 2.4 %pad_maximum_fusion.xr_ref = bf16[34,128,384]{2,1,0:T(8,128)(2,1)S(1)} fusion(bf16[1,128,384]{2,1,0:T(8,128)(2,1)S(1)} %collective-permute-done.1, bf16[32,128,384]{2,1,0:T(8,128)(2,1)} %bitcast.138, bf16[1,128,384]{2,1,0:T(8,128)(2,1)S(1)} %collective-permute-done), kind=kLoop, calls=%fused_computation | loop fusion | flops 3342336 | bytes 6684672 | tf_op jit(solution)/shard_map/concatenate | solution.py:503
  89.6 3.4 %collective-permute-start.2 = (bf16[34,1,384]{2,1,0:T(2,128)(2,1)S(1)}, bf16[34,1,384]{2,1,0:T(2,128)(2,1)S(1)}, u32[]{:S(2)}, u32[]{:S(2)}) collective-permute-start(bf16[34,1,384]{2,1,0:T(2,128)(2,1)S(1)} %get-tuple-element.50), channel_id=1, source_target_pairs={{0,1},{1,2},{2,3},{3,4},{4,5},{5,6},{6,7},{8,9},{9,10},{10,11},{11... | collective-permute-start | bytes 78344 | tf_op jit(solution)/shard_map/ppermute | solution.py:456
  93.0 1.3 collective-permute-start.3
  94.3 0.7 slice_bitcast_fusion.6
  94.9 4.0 %collective-permute-done.3.right_ref = bf16[34,1,384]{2,1,0:T(2,128)(2,1)S(1)} collective-permute-done((bf16[34,1,384]{2,1,0:T(2,128)(2,1)S(1)}, bf16[34,1,384]{2,1,0:T(2,128)(2,1)S(1)}, u32[]{:S(2)}, u32[]{:S(2)}) %collective-permute-start.3) | collective-permute-done | bytes 26144 | tf_op jit(solution)/shard_map/ppermute | solution.py:457
  99.0 0.6 copy-done.16
  99.6 27.1 %conv_states.1 = (f32[32,128,384]{2,1,0:T(8,128)}, bf16[32,128,128]{2,1,0:T(8,128)(2,1)}, bf16[16,128,256]{2,1,0:T(8,128)(2,1)}, bf16[32,16,384]{2,1,0:T(8,128)(...) custom-call(bf16[34,128,384]{2,1,0:T(8,128)(2,1)} %copy-done, ...), custom_call_target="tpu_custom_call" | custom-call | tf_op jit(solution)/shard_map/conv_states/pallas_call | solution.py:417
  126.7 61.2 %inner.1 = (f32[32,128,384]{2,1,0:T(8,128)}, bf16[32,16,384]{2,1,0:T(8,128)(2,1)}, bf16[32,16,384]{2,1,0:T(8,128)(2,1)}, bf16[16,128,384]{2,1,0:T(8,128)(2,1)}, bf16[16,128,384]{2,1,0:T(8,128)(2,1)}) custom-call(f32[32,128,384]{2,1,0:T(8,128)} %get-tuple-element.31.refs_0_, bf16[32,128,128]{2,1,0:T(8,128)(2,1)} %get-tuple-element.32.refs_1_.rc_ref, ...), custom_call_target="tpu_custom_call" | custom-call | tf_op jit(solution)/shard_map/inner/pallas_call | solution.py:417
  187.9 25.4 %finish.1 = bf16[32,128,192]{2,1,0:T(8,128)(2,1)} custom-call(f32[32,128,384]{2,1,0:T(8,128)} %get-tuple-element.42.y_ref, bf16[32,128,128]{2,1,0:T(8,128)(2,1)} %get-tuple-element.32.refs_1_.rc_ref, bf16[16,128,256]{2,1,0:T(8,128)(2,1)} %get-tuple-element.33.refs_2_.cc_ref, f32[32,42,128]{2,1,0:T(8,128)} %pad_maximum_fusion.2.rv_ref.refs_3_, ...), custom_call_target="tpu_custom_call" | custom-call | tf_op jit(solution)/shard_map/finish/pallas_call | solution.py:417
  213.3 3.9 %copy.193 = bf16[32,128,192]{1,2,0:T(8,128)(2,1)} copy(bf16[32,128,192]{2,1,0:T(8,128)(2,1)} %finish.1) | data formatting | bytes 3145728 | tf_op jit(solution)/shard_map/finish/pallas_call | solution.py:417
  (51 shorter events, 0.6 us)
Async XLA Ops:
  4.5 7.5 %copy-start.4 = (f32[4,6,32,128]{3,2,1,0:T(8,128)S(1)}, f32[4,6,32,128]{3,2,1,0:T(8,128)}, u32[]{:S(2)}) copy-start(f32[4,6,32,128]{3,2,1,0:T(8,128)} %param.30) | copy-start | bytes 1179652
  4.5 47.6 %all-to-all-start = ((bf16[1,32,128,194]{2,3,0,1:T(8,128)(2,1)}), bf16[1,32,128,194]{2,3,0,1:T(8,128)(2,1)S(1)}, u32[]{:S(2)}, u32[]{:S(2)}) async-start(bf16[1,32,128,194]{2,3,0,1:T(8,128)(2,1)} %pad_maximum_fusion.1), calls=%async_computation | async-start | bytes 3276800 | tf_op jit(solution)/shard_map/all_to_all | solution.py:478
  17.0 5.6 %copy-start.3 = (f32[256,16,2,6]{0,1,3,2:T(8,128)}, f32[256,16,2,6]{0,1,3,2:T(8,128)S(1)}, u32[]{:S(2)}) copy-start(f32[256,16,2,6]{0,1,3,2:T(8,128)S(1)} %fusion.34) | copy-start | bytes 589828
  21.8 2.2 %copy-start.6 = (f32[16,2,6,256]{3,2,0,1:T(8,128)S(1)}, f32[16,2,6,256]{3,2,0,1:T(8,128)}, u32[]{:S(2)}) copy-start(f32[16,2,6,256]{3,2,0,1:T(8,128)} %copy.177) | copy-start | bytes 589828
  24.0 4.0 %copy-start.5 = (f32[4,6,32,128]{3,2,1,0:T(8,128)S(1)}, f32[4,6,32,128]{3,2,1,0:T(8,128)}, u32[]{:S(2)}) copy-start(f32[4,6,32,128]{3,2,1,0:T(8,128)} %param.30) | copy-start | bytes 1179652
  26.0 2.6 %copy-start.12 = (f32[2,6,32,128]{3,2,1,0:T(8,128)S(1)}, f32[2,6,32,128]{3,2,1,0:T(8,128)}, u32[]{:S(2)}) copy-start(f32[2,6,32,128]{3,2,1,0:T(8,128)} %get-tuple-element.58) | copy-start | bytes 589828
  34.4 2.2 %copy-start.18 = (f32[3,3,384]{2,1,0:T(4,128)S(1)}, f32[3,3,384]{2,1,0:T(4,128)}, u32[]{:S(2)}) copy-start(f32[3,3,384]{2,1,0:T(4,128)} %param.26) | copy-start | bytes 41476
  34.4 7.3 %copy-start.14 = (bf16[384,192]{0,1:T(8,128)(2,1)S(1)}, bf16[384,192]{0,1:T(8,128)(2,1)}, u32[]{:S(2)}) copy-start(bf16[384,192]{0,1:T(8,128)(2,1)} %param.32) | copy-start | bytes 442372
  36.4 11.1 %copy-start.7 = (f32[16,12,256]{2,1,0:T(8,128)S(1)}, f32[16,12,256]{2,1,0:T(8,128)}, u32[]{:S(2)}) copy-start(f32[16,12,256]{2,1,0:T(8,128)} %copy.185) | copy-start | bytes 589828
  36.4 11.1 %copy-start.8 = (f32[16,12,256]{2,1,0:T(8,128)S(1)}, f32[16,12,256]{2,1,0:T(8,128)}, u32[]{:S(2)}) copy-start(f32[16,12,256]{2,1,0:T(8,128)} %copy.186) | copy-start | bytes 589828
  37.2 12.2 %copy-start.9 = (f32[32,12,128]{2,1,0:T(8,128)S(1)}, f32[32,12,128]{2,1,0:T(8,128)}, u32[]{:S(2)}) copy-start(f32[32,12,128]{2,1,0:T(8,128)} %copy.166) | copy-start | bytes 589828
  37.2 12.2 %copy-start.10 = (f32[32,12,128]{2,1,0:T(8,128)S(1)}, f32[32,12,128]{2,1,0:T(8,128)}, u32[]{:S(2)}) copy-start(f32[32,12,128]{2,1,0:T(8,128)} %copy.167) | copy-start | bytes 589828
  37.2 12.2 %copy-start.11 = (f32[32,12,128]{2,1,0:T(8,128)S(1)}, f32[32,12,128]{2,1,0:T(8,128)}, u32[]{:S(2)}) copy-start(f32[32,12,128]{2,1,0:T(8,128)} %copy.168) | copy-start | bytes 589828
  46.5 4.0 %copy-start.13 = (f32[256,16,2,6]{0,3,1,2:T(8,128)S(1)}, f32[256,16,2,6]{0,3,1,2:T(8,128)}, u32[]{:S(2)}) copy-start(f32[256,16,2,6]{0,3,1,2:T(8,128)} %copy.249) | copy-start | bytes 589828
  46.5 4.0 %copy-start.17 = (f32[6,384,1,1]{1,0,2,3:T(8,128)S(1)}, f32[6,384,1,1]{1,0,2,3:T(8,128)}, u32[]{:S(2)}) copy-start(f32[6,384,1,1]{1,0,2,3:T(8,128)} %reshape.382) | copy-start | bytes 27652
  52.1 1.2 copy-start.2
  56.5 2.3 %copy-start.1 = (bf16[32,1,128,194]{3,2,0,1:T(8,128)(2,1)}, bf16[32,1,128,194]{3,2,0,1:T(8,128)(2,1)S(1)}, u32[]{:S(2)}) copy-start(bf16[32,1,128,194]{3,2,0,1:T(8,128)(2,1)S(1)} %copy.190) | copy-start | bytes 4767748
  81.6 3.8 %collective-permute-start = (bf16[1,128,384]{2,1,0:T(8,128)(2,1)S(1)}, bf16[1,128,384]{2,1,0:T(8,128)(2,1)S(1)}, u32[]{:S(2)}, u32[]{:S(2)}) collective-permute-start(bf16[1,128,384]{2,1,0:T(8,128)(2,1)S(1)} %get-tuple-element.51), channel_id=1, source_target_pairs={{0,8},{8,16},{16,24},{1,9},{9,17},{17,25},{2,10},{10,18},{18,26},{... | collective-permute-start | bytes 294920 | tf_op jit(solution)/shard_map/ppermute | solution.py:456
  83.2 3.9 %collective-permute-start.1 = (bf16[1,128,384]{2,1,0:T(8,128)(2,1)S(1)}, bf16[1,128,384]{2,1,0:T(8,128)(2,1)S(1)}, u32[]{:S(2)}, u32[]{:S(2)}) collective-permute-start(bf16[1,128,384]{2,1,0:T(8,128)(2,1)S(1)} %get-tuple-element.52), channel_id=1, source_target_pairs={{8,0},{16,8},{24,16},{9,1},{17,9},{25,17},{10,2},{18,10},{26,18},{... | collective-permute-start | bytes 294920 | tf_op jit(solution)/shard_map/ppermute | solution.py:457
  89.5 9.5 %copy-start = (bf16[34,128,384]{2,1,0:T(8,128)(2,1)}, bf16[34,128,384]{2,1,0:T(8,128)(2,1)S(1)}, u32[]{:S(2)}) copy-start(bf16[34,128,384]{2,1,0:T(8,128)(2,1)S(1)} %pad_maximum_fusion.xr_ref) | copy-start | bytes 10027012
  89.6 5.4 %collective-permute-start.2 = (bf16[34,1,384]{2,1,0:T(2,128)(2,1)S(1)}, bf16[34,1,384]{2,1,0:T(2,128)(2,1)S(1)}, u32[]{:S(2)}, u32[]{:S(2)}) collective-permute-start(bf16[34,1,384]{2,1,0:T(2,128)(2,1)S(1)} %get-tuple-element.50), channel_id=1, source_target_pairs={{0,1},{1,2},{2,3},{3,4},{4,5},{5,6},{6,7},{8,9},{9,10},{10,11},{11... | collective-permute-start | bytes 78344 | tf_op jit(solution)/shard_map/ppermute | solution.py:456
  93.0 6.0 %collective-permute-start.3 = (bf16[34,1,384]{2,1,0:T(2,128)(2,1)S(1)}, bf16[34,1,384]{2,1,0:T(2,128)(2,1)S(1)}, u32[]{:S(2)}, u32[]{:S(2)}) collective-permute-start(bf16[34,1,384]{2,1,0:T(2,128)(2,1)S(1)} %get-tuple-element.49), channel_id=1, source_target_pairs={{1,0},{2,1},{3,2},{4,3},{5,4},{6,5},{7,6},{9,8},{10,9},{11,10},{12... | collective-permute-start | bytes 78344 | tf_op jit(solution)/shard_map/ppermute | solution.py:457
  94.9 4.0 %copy-start.15 = (bf16[34,1,384]{2,1,0:T(2,128)(2,1)}, bf16[34,1,384]{2,1,0:T(2,128)(2,1)S(1)}, u32[]{:S(2)}) copy-start(bf16[34,1,384]{2,1,0:T(2,128)(2,1)S(1)} %collective-permute-done.2.left_ref) | copy-start | bytes 78340
  99.0 0.6 copy-start.16

commit v3 on v2

--- a/solution.py
+++ b/solution.py
@@ -33,20 +33,25 @@
     return v * lax.rsqrt(jnp.mean(v * v, axis=-1, keepdims=True) + 1e-06) * gains
 
 
-def place_kernel(cells_ref, values_ref, gain_ref, w_ref, grid_ref, x_ref, z_ref):
+def place_kernel(values_ref, gain_ref, w_ref, grid_ref, x_ref, z_ref):
     tile, channels = grid_ref.shape
-    slots = values_ref.shape[0]
-    chunk = min(slots, 1024)
+    loaders, _, slots = values_ref.shape
+    together = 8
     base = pl.program_id(0) * tile
-    ids = base + lax.broadcasted_iota(jnp.int32, (tile, chunk), 0)
+    ids = base + lax.broadcasted_iota(jnp.int32, (tile, together * slots), 0)
 
     def add(k, acc):
-        at = pl.ds(pl.multiple_of(k * chunk, chunk), chunk)
-        hot = jnp.where(ids == cells_ref[:, at], 1.0, 0.0).astype(BF)
-        return acc + dot(hot, values_ref[at, :])
-
-    acc = lax.fori_loop(0, slots // chunk, add, jnp.zeros((tile, values_ref.shape[1]), F32))
-    acc = acc[:, :channels]
+        held = jnp.concatenate([values_ref[k * together + i] for i in range(together)], axis=1)
+        named = held[channels:, :].astype(F32)
+        cell = (named[0:1] * LANES + named[1:2]).astype(jnp.int32)
+        hot = jnp.where(ids == cell, 1.0, 0.0).astype(BF)
+        return acc + lax.dot_general(
+            hot, held[:channels], (((1,), (1,)), ((), ())), preferred_element_type=F32
+        )
+
+    acc = lax.fori_loop(
+        0, loaders // together, add, jnp.zeros((tile, channels), F32), unroll=2
+    )
     grid_ref[...] = acc.astype(BF)
     normed = rms(acc, gain_ref[...]).astype(BF)
     both = dot(normed, w_ref[...]).astype(BF)
@@ -55,12 +60,12 @@
     z_ref[...] = both[:, width:]
 
 
-def place(cells, values, gain, w, n_cells):
+def place(values, gain, w, n_cells):
     channels, width = w.shape[0], w.shape[1] // 2
     tile = 512
 
     def whole(shape):
-        return pl.BlockSpec(shape, lambda i: (0, 0))
+        return pl.BlockSpec(shape, lambda i: (0,) * len(shape))
 
     def rows(n):
         return pl.BlockSpec((tile, n), lambda i: (i, 0))
@@ -68,7 +73,7 @@
     return pl.pallas_call(
         place_kernel,
         grid=(n_cells // tile,),
-        in_specs=[whole(cells.shape), whole(values.shape), whole(gain.shape), whole(w.shape)],
+        in_specs=[whole(values.shape), whole(gain.shape), whole(w.shape)],
         out_specs=[rows(channels), rows(width), rows(width)],
         out_shape=[
             jax.ShapeDtypeStruct((n_cells, channels), BF),
@@ -77,7 +82,7 @@
         ],
         compiler_params=pltpu.CompilerParams(**PARAMS),
         name="place",
-    )(cells, values, gain, w)
+    )(values, gain, w)
 
 
 def lane_low(shape):
@@ -159,9 +164,9 @@
     return lambda i: ref[g, i : i + 1, :]
 
 
-def conv_kernel(
-    heads, state, xr_ref, left_ref, right_ref, w_ref, bias_ref, proj_ref, rv_ref, cv_ref,
-    x_ref, rc_ref, cc_ref, f0_ref, f1_ref, f2_ref, f3_ref,
+def conv_rows(
+    heads, state, xr_ref, left_ref, right_ref, w_ref, bias_ref, proj_ref, rv_ref,
+    x_ref, rc_ref, f0_ref, f1_ref,
 ):
     rows_n, cols_n, width = x_ref.shape
     place = lax.broadcasted_iota(jnp.int32, (cols_n, LANES), 0)
@@ -195,19 +200,16 @@
 
     lax.fori_loop(0, rows_n, one_row, 0, unroll=2)
 
-    def one_group(g, carry):
-        x = x_ref[:, pl.ds(pl.multiple_of(g * GROUP, GROUP), GROUP), :]
-        x = x.reshape(rows_n * GROUP, width).astype(BF)
-        coefs = lax.dot_general(
-            proj_ref[...], x, (((0,), (1,)), ((), ())), preferred_element_type=F32
-        ).astype(BF)
-        cc_ref[g] = coefs
-        states(
-            x, coefs, 1, row_of(cv_ref, g), heads, state, GROUP, (f2_ref.at[g], f3_ref.at[g])
-        )
-        return carry
-
-    lax.fori_loop(0, cols_n // GROUP, one_group, 0, unroll=2)
+
+def column_states(heads, state, g, proj_ref, cv_ref, x_ref, cc_ref, f2_ref, f3_ref):
+    rows_n, _, width = x_ref.shape
+    x = x_ref[:, pl.ds(pl.multiple_of(g * GROUP, GROUP), GROUP), :]
+    x = x.reshape(rows_n * GROUP, width).astype(BF)
+    coefs = lax.dot_general(
+        proj_ref[...], x, (((0,), (1,)), ((), ())), preferred_element_type=F32
+    ).astype(BF)
+    cc_ref[g] = coefs
+    states(x, coefs, 1, row_of(cv_ref, g), heads, state, GROUP, (f2_ref.at[g], f3_ref.at[g]))
 
 
 def hop(what, axis, reverse, k, part, final_ref, decay_ref, enter_ref, land_ref, send_ref, sems):
@@ -289,12 +291,14 @@
 
 
 def inner_kernel(heads, state, *refs):
-    x_ref, rc_ref, cc_ref, rv_ref, cv_ref, ra_ref, ca_ref, skip_ref = refs[:8]
-    finals, decays, (y_ref,), enters = refs[8:12], refs[12:16], refs[16:17], refs[17:21]
-    lands, sends, sems = refs[21:25], refs[25:29], refs[29:]
+    xr_ref, left_ref, right_ref, w_ref, bias_ref, proj_ref, rv_ref, cv_ref, ra_ref, ca_ref, skip_ref = refs[:11]
+    decays, (y_ref, rc_ref, cc_ref), enters = refs[11:15], refs[15:18], refs[18:22]
+    x_ref, finals, lands, sends, sems = refs[22], refs[23:27], refs[27:31], refs[31:35], refs[35:]
     rows_n, cols_n, width = x_ref.shape
     row_steps = rows_n // 2
-    steps = row_steps + cols_n // GROUP
+    groups = cols_n // GROUP
+    state_steps = groups // 2
+    steps = state_steps + row_steps + groups
     ways = (("col", False), ("col", True), ("row", False), ("row", True))
 
     def pass_on(what, k, part):
@@ -307,11 +311,15 @@
         axis, reverse = ways[k]
         count, index = lax.axis_size(axis), lax.axis_index(axis)
         turn = count - 1 - index if reverse else index
-        apart, each = (2, 3) if axis == "col" else (3, 4)
-        each = max(1, min(each, (steps - 1 - (PARTS - 1) * apart) // max(1, count - 1)))
-        return turn * each + part * apart
+        begin, apart, each = (0, 2, 4) if axis == "col" else (state_steps // PARTS, 3, 4)
+        each = max(1, min(each, (steps - 1 - begin - (PARTS - 1) * apart) // max(1, count - 1)))
+        return begin + turn * each + part * apart
 
     greet(("row", "col"))
+    conv_rows(
+        heads, state, xr_ref, left_ref, right_ref, w_ref, bias_ref, proj_ref, rv_ref,
+        x_ref, rc_ref, finals[0], finals[1],
+    )
 
     def two_rows(s):
         done = []
@@ -342,13 +350,20 @@
                 def _(k=k, part=part):
                     pass_on("hop", k, part)
 
-        @pl.when(s < row_steps)
+        @pl.when(s < state_steps)
         def _():
-            two_rows(s)
-
-        @pl.when(s >= row_steps)
+            for i in range(2):
+                column_states(
+                    heads, state, 2 * s + i, proj_ref, cv_ref, x_ref, cc_ref, finals[2], finals[3]
+                )
+
+        @pl.when((s >= state_steps) & (s < state_steps + row_steps))
         def _():
-            one_group(s - row_steps)
+            two_rows(s - state_steps)
+
+        @pl.when(s >= state_steps + row_steps)
+        def _():
+            one_group(s - state_steps - row_steps)
 
         return carry
 
@@ -363,7 +378,7 @@
     z_ref, grid_ref, gain_ref, out_w_ref, mlp_gain_ref, ff_in_ref, ff_out_ref, out_ref, sum_ref, held_ref, sem,
 ):
     rows_n, cols_n, width = y_ref.shape
-    channels = out_ref.shape[2]
+    channels = out_ref.shape[1]
     span = SPAN
 
     def leave(s):
@@ -400,7 +415,8 @@
         v = dot(normed, ff_in_ref[...])
         hidden = (v * 0.5 * (1.0 + lax.erf(v * 0.7071067811865476))).astype(BF)
         out = dot(hidden, ff_out_ref[...]) + middle
-        held_ref[here] = out.astype(BF).reshape(span, cols_n, channels)
+        for i in range(span):
+            held_ref[s * span + i] = out[i * cols_n : (i + 1) * cols_n].T.astype(BF)
         leave(s).start()
         return carry
 
@@ -484,17 +500,11 @@
         decay_rate[2:].reshape(2, heads, rows_n, groups, GROUP), (3, 0, 1, 2, 4)
     ).reshape(groups, 2, heads, rows_n * GROUP)
     cv, ca, cd = rate_vectors(cols_first, GROUP, per_head)
+    got = jnp.swapaxes(got.reshape(-1, slots, channels + 2), 1, 2)
     got, rv, ra, rd, cv, ca, cd = lax.optimization_barrier((got, rv, ra, rd, cv, ca, cd))
 
-    got = got.reshape(-1, channels + 2)
-    got_cells = got[:, channels:].astype(jnp.int32)
-    got_cells = got_cells[:, 0] * LANES + got_cells[:, 1]
     grid, inner_x, gate = place(
-        got_cells.reshape(1, -1),
-        got,
-        norm_gain[None],
-        jnp.concatenate([in_x, in_z], axis=1),
-        cells,
+        got, norm_gain[None], jnp.concatenate([in_x, in_z], axis=1), cells
     )
     grid = grid.reshape(rows_n, cols_n, channels)
     gate = gate.reshape(rows_n, cols_n, width)
@@ -505,44 +515,43 @@
 
     one_row = jax.ShapeDtypeStruct((rows_n, state, width), BF)
     one_col = jax.ShapeDtypeStruct((groups, GROUP * state, width), BF)
-    x, rc, cc, f0, f1, f2, f3 = call(
-        functools.partial(conv_kernel, heads, state),
-        "conv_states",
-        (tall, left, right, conv_w.reshape(9, width), conv_bias[None], x_proj, rv, cv),
+    passed = [one_row, one_row, one_col, one_col]
+    slots_of = [pltpu.VMEM(shape.shape, shape.dtype) for shape in passed]
+    y, rc, cc, e0, e1, e2, e3 = call(
+        functools.partial(inner_kernel, heads, state),
+        "conv_scan",
+        (
+            tall, left, right, conv_w.reshape(9, width), conv_bias[None], x_proj, rv, cv, ra, ca,
+            skip_gain[None], rd[0], rd[1], cd[0], cd[1],
+        ),
         [
             jax.ShapeDtypeStruct((rows_n, cols_n, width), F32),
             jax.ShapeDtypeStruct((rows_n, x_proj.shape[1], cols_n), BF),
             jax.ShapeDtypeStruct((groups, x_proj.shape[1], rows_n * GROUP), BF),
-            one_row, one_row, one_col, one_col,
-        ],
-    )
-
-    passed = [one_row, one_row, one_col, one_col]
-    slots_of = [pltpu.VMEM(shape.shape, shape.dtype) for shape in passed]
-    y, e0, e1, e2, e3 = call(
-        functools.partial(inner_kernel, heads, state),
-        "inner",
-        (x, rc, cc, rv, cv, ra, ca, skip_gain[None], f0, f1, f2, f3, rd[0], rd[1], cd[0], cd[1]),
-        [jax.ShapeDtypeStruct((rows_n, cols_n, width), F32)] + passed,
-        scratch=slots_of + slots_of + [pltpu.SemaphoreType.DMA((4 * PARTS,))] * 2,
+        ]
+        + passed,
+        scratch=[pltpu.VMEM((rows_n, cols_n, width), F32)]
+        + slots_of * 3
+        + [pltpu.SemaphoreType.DMA((4 * PARTS,))] * 2,
         collective_id=0,
         has_side_effects=True,
     )
-    return call(
+    out = call(
         functools.partial(finish_kernel, heads, state),
         "finish",
         (
             y, rc, cc, rv, cv, e0, e1, e2, e3, gate, grid, out_gain[None], out_w,
             mlp_gain[None], ff_in, ff_out,
         ),
-        [jax.ShapeDtypeStruct((rows_n, cols_n, channels), BF)],
+        [jax.ShapeDtypeStruct((rows_n, channels, cols_n), BF)],
         scratch=[
             pltpu.VMEM((rows_n, cols_n, width), F32),
-            pltpu.VMEM((rows_n, cols_n, channels), BF),
+            pltpu.VMEM((rows_n, channels, cols_n), BF),
             pltpu.SemaphoreType.DMA((rows_n // SPAN,)),
         ],
         out_space=pl.ANY,
     )[0]
+    return jnp.swapaxes(out, 1, 2)
 
 
 def solution(mesh):

time: 218 us -> 192 us (0.88)
  Pallas kernels: 136 us -> 120 us
  local copies, waits for them, and re-layouts: 38.4 us -> 26.7 us
  waiting for transfers between devices: 6.71 us -> 12.8 us
  other arithmetic: 16.4 us -> 13.3 us
    pallas_call x3 -> x2, Pallas kernels: 114 us -> 102 us  [call(): pl.pallas_call(kernel, in_specs=[VMEM] * len(args), out_specs=[pl.BlockSp...]
    all_to_all x1, waiting for transfers between devices: 1.07 us -> 7.14 us  [local(): lax.all_to_all(sent, ('row', 'col'), split_axis=1, concat_axis=0, tiled=T...]
    pallas_call x1 -> x0, local copies, waits for them, and re-layouts: 3.93 us -> none  [call(): pl.pallas_call(kernel, in_specs=[VMEM] * len(args), out_specs=[pl.BlockSp...]
    pallas_call x1, Pallas kernels: 21.9 us -> 18.6 us  [place(): pl.pallas_call(place_kernel, grid=(n_cells // tile,), in_specs=[whole(val...]
    optimization_barrier x1 -> x0, local copies, waits for them, and re-layouts: 3.16 us -> none  [local(): lax.optimization_barrier((got, rv, ra, rd, cv, ca, cd))]
    unnamed x41 -> x51, local copies, waits for them, and re-layouts: 5.73 us -> 4.8 us
  transfers between devices with their start and end apart: 5 -> 5, of which waited for: 3 -> 3; matrix products, arithmetic and copies ran while one was open for 19% -> 18% of each run, Pallas kernels for 0% -> 0%
where the time goes in v3:
time: 192 us
  Pallas kernels  120 us (62%)
  local copies, waits for them, and re-layouts  26.7 us (14%)
  starting transfers between devices  14 us (7%)
  other arithmetic  13.3 us (7%)
  waiting for transfers between devices  12.8 us (7%)
  matrix products  4.01 us (2%)
    pallas_call x2, Pallas kernels, call(): pl.pallas_call(kernel, in_specs=[VMEM] * len(args), out_specs=[pl.BlockSp...  102 us
    pallas_call x1, Pallas kernels, place(): pl.pallas_call(place_kernel, grid=(n_cells // tile,), in_specs=[whole(val...  18.6 us
    all_to_all x1, starting transfers between devices, local(): lax.all_to_all(sent, ('row', 'col'), split_axis=1, concat_axis=0, tiled=T...  7.3 us
    all_to_all x1, waiting for transfers between devices, local(): lax.all_to_all(sent, ('row', 'col'), split_axis=1, concat_axis=0, tiled=T...  7.14 us
    ppermute x2, waiting for transfers between devices, halo(): high = lax.ppermute(lax.slice_in_dim(block, 0, 1, axis=dim), axis, backward)  5.65 us
    unnamed x51, local copies, waits for them, and re-layouts  4.8 us
    ppermute x2, starting transfers between devices, halo(): lax.ppermute(lax.slice_in_dim(block, n - 1, n, axis=dim), axis, forward)  4.15 us
    reshape x2, local copies, waits for them, and re-layouts, rate_vectors(): return (vecs, jnp.swapaxes(cum.reshape(both), 1, 2), decay)  3.94 us
  transfers between devices with their start and end apart: 5, of which 3 were waited for; matrix products, arithmetic and copies ran while one was open for 18% of the time, Pallas kernels for 0%

profile of v3, /device:TPU:0, one launch (start us, length us, event | category | flops | bytes accessed | tf_op | source)
XLA Modules:
  0.0 191.5 jit_solution(12190563201897373264)
XLA Ops:
  0.0 0.8 fusion.57
  0.9 0.7 compare_bitcast_fusion
  1.6 1.6 bitcast_select_fusion
  3.2 1.3 pad_maximum_fusion.1
  4.5 7.3 %all-to-all-start = ((bf16[1,32,128,194]{2,3,0,1:T(8,128)(2,1)}), bf16[1,32,128,194]{2,3,0,1:T(8,128)(2,1)S(1)}, u32[]{:S(2)}, u32[]{:S(2)}) async-start(bf16[1,32,128,194]{2,3,0,1:T(8,128)(2,1)} %pad_maximum_fusion.1), calls=%async_computation | async-start | bytes 3276800 | tf_op jit(solution)/shard_map/all_to_all | solution.py:494
  11.8 0.2 fusion.30
  12.1 0.7 fusion.70
  12.8 1.2 copy.192
  13.9 1.7 copy.164
  15.6 1.4 fusion.33
  17.0 0.7 broadcast_in_dim.51
  17.7 1.4 reshape.359
  19.1 0.8 reshape.356
  19.9 1.3 copy.167
  21.2 0.8 copy.237
  22.0 1.4 fusion
  23.4 0.0 copy-done.3
  23.4 1.1 bitcast_add_fusion
  24.5 0.1 copy.169
  24.5 0.1 copy.174
  24.7 0.1 copy.172
  24.7 0.8 copy.175
  25.6 0.1 copy.173
  25.6 0.8 copy.176
  26.4 0.2 fusion.39
  26.7 0.1 copy.238
  26.8 0.2 fusion.37
  27.1 1.2 bitcast_add_fusion.1
  28.3 0.8 copy.156
  29.2 0.8 copy.157
  30.1 0.8 copy.158
  30.9 2.0 %copy.178 = f32[16,12,256]{1,2,0:T(8,128)} copy(f32[16,12,256]{2,0,1:T(8,128)S(1)} %bitcast.142) | data formatting | bytes 393216 | tf_op jit(solution)/shard_map/reshape | solution.py:464
  32.9 2.0 %copy.160 = f32[32,12,128]{1,2,0:T(8,128)} copy(f32[32,12,128]{2,0,1:T(8,128)S(1)} %bitcast.141) | data formatting | bytes 393216 | tf_op jit(solution)/shard_map/reshape | solution.py:464
  34.9 0.2 copy.161
  35.1 0.6 reshape.351.refs_3_
  35.7 0.5 broadcast_in_dim.53.refs_4_
  36.2 0.6 broadcast_in_dim.54.refs_10_
  36.8 0.9 copy.181.ff_out_ref
  37.8 0.8 copy.180.out_w_ref
  38.6 0.5 broadcast_in_dim.55.gain_ref
  39.2 0.3 fusion.55
  39.5 0.1 reshape_bitcast_fusion
  39.5 1.7 pad_maximum_fusion.4.w_ref
  41.3 0.9 slice_bitcast_fusion.2
  42.2 1.1 pad_maximum_fusion.3.refs_7_.cv_ref
  43.3 1.1 pad_maximum_fusion.2.refs_6_.rv_ref
  44.4 0.5 convolution_bitcast_fusion
  44.9 7.1 %all-to-all-done = bf16[1,32,128,194]{2,3,0,1:T(8,128)(2,1)S(1)} async-done(((bf16[1,32,128,194]{2,3,0,1:T(8,128)(2,1)}), bf16[1,32,128,194]{2,3,0,1:T(8,128)(2,1)S(1)}, u32[]{:S(2)}, u32[]{:S(2)}) %all-to-all-start) | async-done | bytes 1589280 | tf_op jit(solution)/shard_map/all_to_all | solution.py:494
  52.1 1.2 copy-done.1
  53.2 18.6 %place.1 = (bf16[4096,192]{1,0:T(8,128)(2,1)}, bf16[4096,384]{1,0:T(8,128)(2,1)}, bf16[4096,384]{1,0:T(8,128)(2,1)}) custom-call(bf16[32,194,128]{2,1,0:T(8,128)(2,1)} %bitcast.136, f32[1,192]{1,0:T(1,128)} %bitcast.152, bf16[192,768]{1,0:T(8,128)(2,1)} %pad_maximum_fusion.4.w_ref), custom_call_target="tpu_custom_call" | custom-call | tf_op jit(solution)/shard_map/place/pallas_call | solution.py:73
  71.8 1.0 slice_bitcast_fusion.5
  72.8 1.6 collective-permute-start
  74.4 1.3 collective-permute-start.1
  75.7 0.8 slice_bitcast_fusion
  76.4 1.6 collective-permute-done.1
  78.1 2.4 %pad_maximum_fusion.refs_0_ = bf16[34,128,384]{2,1,0:T(8,128)(2,1)S(1)} fusion(bf16[1,128,384]{2,1,0:T(8,128)(2,1)S(1)} %collective-permute-done.1, bf16[32,128,384]{2,1,0:T(8,128)(2,1)} %bitcast.137, bf16[1,128,384]{2,1,0:T(8,128)(2,1)S(1)} %collective-permute-done), kind=kLoop, calls=%fused_computation | loop fusion | flops 3342336 | bytes 6684672 | tf_op jit(solution)/shard_map/concatenate | solution.py:513
  80.5 0.1 fusion.69
  80.6 2.6 %collective-permute-start.2 = (bf16[34,1,384]{2,1,0:T(2,128)(2,1)S(1)}, bf16[34,1,384]{2,1,0:T(2,128)(2,1)S(1)}, u32[]{:S(2)}, u32[]{:S(2)}) collective-permute-start(bf16[34,1,384]{2,1,0:T(2,128)(2,1)S(1)} %get-tuple-element.40), channel_id=1, source_target_pairs={{0,1},{1,2},{2,3},{3,4},{4,5},{5,6},{6,7},{8,9},{9,10},{10,11},{11... | collective-permute-start | bytes 78344 | tf_op jit(solution)/shard_map/ppermute | solution.py:472
  83.1 1.3 collective-permute-start.3
  84.4 0.7 slice_bitcast_fusion.6
  85.1 4.0 %collective-permute-done.3.refs_2_ = bf16[34,1,384]{2,1,0:T(2,128)(2,1)S(1)} collective-permute-done((bf16[34,1,384]{2,1,0:T(2,128)(2,1)S(1)}, bf16[34,1,384]{2,1,0:T(2,128)(2,1)S(1)}, u32[]{:S(2)}, u32[]{:S(2)}) %collective-permute-start.3) | collective-permute-done | bytes 26144 | tf_op jit(solution)/shard_map/ppermute | solution.py:473
  89.2 0.6 copy-done.18
  89.8 75.6 %conv_scan.1 = (f32[32,128,384]{2,1,0:T(8,128)}, bf16[32,128,128]{2,1,0:T(8,128)(2,1)}, bf16[16,128,256]{2,1,0:T(8,128)(2,1)}, bf16[32,16,384]{2,1,0:T(8,128)(2,...) custom-call(bf16[34,128,384]{2,1,0:T(8,128)(2,1)} %copy-done, ...), custom_call_target="tpu_custom_call" | custom-call | tf_op jit(solution)/shard_map/conv_scan/pallas_call | solution.py:433
  165.4 25.9 %finish.1 = bf16[32,192,128]{2,1,0:T(8,128)(2,1)} custom-call(f32[32,128,384]{2,1,0:T(8,128)} %get-tuple-element.30.y_ref, bf16[32,128,128]{2,1,0:T(8,128)(2,1)} %get-tuple-element.31.rc_ref, bf16[16,128,256]{2,1,0:T(8,128)(2,1)} %get-tuple-element.32.cc_ref, f32[32,42,128]{2,1,0:T(8,128)} %pad_maximum_fusion.2.refs_6_.rv_ref, ...), custom_call_target="tpu_custom_call" | custom-call | tf_op jit(solution)/shard_map/finish/pallas_call | solution.py:433
  (56 shorter events, 0.3 us)
Async XLA Ops:
  4.5 7.5 %copy-start.4 = (f32[4,6,32,128]{3,2,1,0:T(8,128)S(1)}, f32[4,6,32,128]{3,2,1,0:T(8,128)}, u32[]{:S(2)}) copy-start(f32[4,6,32,128]{3,2,1,0:T(8,128)} %param.30) | copy-start | bytes 1179652
  4.5 47.6 %all-to-all-start = ((bf16[1,32,128,194]{2,3,0,1:T(8,128)(2,1)}), bf16[1,32,128,194]{2,3,0,1:T(8,128)(2,1)S(1)}, u32[]{:S(2)}, u32[]{:S(2)}) async-start(bf16[1,32,128,194]{2,3,0,1:T(8,128)(2,1)} %pad_maximum_fusion.1), calls=%async_computation | async-start | bytes 3276800 | tf_op jit(solution)/shard_map/all_to_all | solution.py:494
  17.0 5.0 %copy-start.2 = (f32[256,16,2,6]{0,1,3,2:T(8,128)}, f32[256,16,2,6]{0,1,3,2:T(8,128)S(1)}, u32[]{:S(2)}) copy-start(f32[256,16,2,6]{0,1,3,2:T(8,128)S(1)} %fusion.33) | copy-start | bytes 589828
  21.2 2.2 %copy-start.6 = (f32[16,2,6,256]{3,2,0,1:T(8,128)S(1)}, f32[16,2,6,256]{3,2,0,1:T(8,128)}, u32[]{:S(2)}) copy-start(f32[16,2,6,256]{3,2,0,1:T(8,128)} %copy.167) | copy-start | bytes 589828
  22.0 1.4 copy-start.3
  24.5 2.0 %copy-start.5 = (f32[4,6,32,128]{3,2,1,0:T(8,128)S(1)}, f32[4,6,32,128]{3,2,1,0:T(8,128)}, u32[]{:S(2)}) copy-start(f32[4,6,32,128]{3,2,1,0:T(8,128)} %param.30) | copy-start | bytes 1179652
  24.7 2.4 %copy-start.12 = (f32[2,6,32,128]{3,2,1,0:T(8,128)S(1)}, f32[2,6,32,128]{3,2,1,0:T(8,128)}, u32[]{:S(2)}) copy-start(f32[2,6,32,128]{3,2,1,0:T(8,128)} %get-tuple-element.48) | copy-start | bytes 589828
  32.9 2.2 %copy-start.20 = (f32[3,3,384]{2,1,0:T(4,128)S(1)}, f32[3,3,384]{2,1,0:T(4,128)}, u32[]{:S(2)}) copy-start(f32[3,3,384]{2,1,0:T(4,128)} %param.26) | copy-start | bytes 41476
  32.9 2.8 %copy-start.21 = (f32[384]{0:T(512)S(1)}, f32[384]{0:T(512)}, u32[]{:S(2)}) copy-start(f32[384]{0:T(512)} %param.27) | copy-start | bytes 4612
  32.9 3.4 %copy-start.22 = (f32[384]{0:T(512)S(1)}, f32[384]{0:T(512)}, u32[]{:S(2)}) copy-start(f32[384]{0:T(512)} %param.29) | copy-start | bytes 4612
  32.9 4.0 %copy-start.15 = (bf16[768,192]{0,1:T(8,128)(2,1)S(1)}, bf16[768,192]{0,1:T(8,128)(2,1)}, u32[]{:S(2)}) copy-start(bf16[768,192]{0,1:T(8,128)(2,1)} %param.35) | copy-start | bytes 884740
  32.9 4.9 %copy-start.16 = (bf16[384,192]{0,1:T(8,128)(2,1)S(1)}, bf16[384,192]{0,1:T(8,128)(2,1)}, u32[]{:S(2)}) copy-start(bf16[384,192]{0,1:T(8,128)(2,1)} %param.32) | copy-start | bytes 442372
  32.9 5.7 %copy-start.23 = (f32[384]{0:T(512)S(1)}, f32[384]{0:T(512)}, u32[]{:S(2)}) copy-start(f32[384]{0:T(512)} %param.31) | copy-start | bytes 4612
  34.9 7.3 %copy-start.7 = (f32[16,12,256]{2,1,0:T(8,128)S(1)}, f32[16,12,256]{2,1,0:T(8,128)}, u32[]{:S(2)}) copy-start(f32[16,12,256]{2,1,0:T(8,128)} %copy.175) | copy-start | bytes 589828
  34.9 7.3 %copy-start.8 = (f32[16,12,256]{2,1,0:T(8,128)S(1)}, f32[16,12,256]{2,1,0:T(8,128)}, u32[]{:S(2)}) copy-start(f32[16,12,256]{2,1,0:T(8,128)} %copy.176) | copy-start | bytes 589828
  37.8 5.5 %copy-start.13 = (f32[32,2,6,128]{3,2,0,1:T(8,128)S(1)}, f32[32,2,6,128]{3,2,0,1:T(8,128)}, u32[]{:S(2)}) copy-start(f32[32,2,6,128]{3,2,0,1:T(8,128)} %get-tuple-element.53) | copy-start | bytes 589828
  38.6 4.7 %copy-start.9 = (f32[32,12,128]{2,1,0:T(8,128)S(1)}, f32[32,12,128]{2,1,0:T(8,128)}, u32[]{:S(2)}) copy-start(f32[32,12,128]{2,1,0:T(8,128)} %copy.156) | copy-start | bytes 589828
  38.6 4.7 %copy-start.10 = (f32[32,12,128]{2,1,0:T(8,128)S(1)}, f32[32,12,128]{2,1,0:T(8,128)}, u32[]{:S(2)}) copy-start(f32[32,12,128]{2,1,0:T(8,128)} %copy.157) | copy-start | bytes 589828
  38.6 4.7 %copy-start.11 = (f32[32,12,128]{2,1,0:T(8,128)S(1)}, f32[32,12,128]{2,1,0:T(8,128)}, u32[]{:S(2)}) copy-start(f32[32,12,128]{2,1,0:T(8,128)} %copy.158) | copy-start | bytes 589828
  42.2 2.2 %copy-start.14 = (f32[256,16,2,6]{0,3,1,2:T(8,128)S(1)}, f32[256,16,2,6]{0,3,1,2:T(8,128)}, u32[]{:S(2)}) copy-start(f32[256,16,2,6]{0,3,1,2:T(8,128)} %copy.237) | copy-start | bytes 589828
  42.2 2.2 %copy-start.19 = (f32[6,384,1,1]{1,0,2,3:T(8,128)S(1)}, f32[6,384,1,1]{1,0,2,3:T(8,128)}, u32[]{:S(2)}) copy-start(f32[6,384,1,1]{1,0,2,3:T(8,128)} %reshape.359) | copy-start | bytes 27652
  52.1 1.2 copy-start.1
  72.8 3.6 %collective-permute-start = (bf16[1,128,384]{2,1,0:T(8,128)(2,1)S(1)}, bf16[1,128,384]{2,1,0:T(8,128)(2,1)S(1)}, u32[]{:S(2)}, u32[]{:S(2)}) collective-permute-start(bf16[1,128,384]{2,1,0:T(8,128)(2,1)S(1)} %get-tuple-element.41), channel_id=1, source_target_pairs={{0,8},{8,16},{16,24},{1,9},{9,17},{17,25},{2,10},{10,18},{18,26},{... | collective-permute-start | bytes 294920 | tf_op jit(solution)/shard_map/ppermute | solution.py:472
  74.4 3.7 %collective-permute-start.1 = (bf16[1,128,384]{2,1,0:T(8,128)(2,1)S(1)}, bf16[1,128,384]{2,1,0:T(8,128)(2,1)S(1)}, u32[]{:S(2)}, u32[]{:S(2)}) collective-permute-start(bf16[1,128,384]{2,1,0:T(8,128)(2,1)S(1)} %get-tuple-element.42), channel_id=1, source_target_pairs={{8,0},{16,8},{24,16},{9,1},{17,9},{25,17},{10,2},{18,10},{26,18},{... | collective-permute-start | bytes 294920 | tf_op jit(solution)/shard_map/ppermute | solution.py:473
  80.5 8.7 %copy-start = (bf16[34,128,384]{2,1,0:T(8,128)(2,1)}, bf16[34,128,384]{2,1,0:T(8,128)(2,1)S(1)}, u32[]{:S(2)}) copy-start(bf16[34,128,384]{2,1,0:T(8,128)(2,1)S(1)} %pad_maximum_fusion.refs_0_) | copy-start | bytes 10027012
  80.6 4.6 %collective-permute-start.2 = (bf16[34,1,384]{2,1,0:T(2,128)(2,1)S(1)}, bf16[34,1,384]{2,1,0:T(2,128)(2,1)S(1)}, u32[]{:S(2)}, u32[]{:S(2)}) collective-permute-start(bf16[34,1,384]{2,1,0:T(2,128)(2,1)S(1)} %get-tuple-element.40), channel_id=1, source_target_pairs={{0,1},{1,2},{2,3},{3,4},{4,5},{5,6},{6,7},{8,9},{9,10},{10,11},{11... | collective-permute-start | bytes 78344 | tf_op jit(solution)/shard_map/ppermute | solution.py:472
  83.1 6.0 %collective-permute-start.3 = (bf16[34,1,384]{2,1,0:T(2,128)(2,1)S(1)}, bf16[34,1,384]{2,1,0:T(2,128)(2,1)S(1)}, u32[]{:S(2)}, u32[]{:S(2)}) collective-permute-start(bf16[34,1,384]{2,1,0:T(2,128)(2,1)S(1)} %get-tuple-element.39), channel_id=1, source_target_pairs={{1,0},{2,1},{3,2},{4,3},{5,4},{6,5},{7,6},{9,8},{10,9},{11,10},{12... | collective-permute-start | bytes 78344 | tf_op jit(solution)/shard_map/ppermute | solution.py:473
  85.1 4.0 %copy-start.17 = (bf16[34,1,384]{2,1,0:T(2,128)(2,1)}, bf16[34,1,384]{2,1,0:T(2,128)(2,1)S(1)}, u32[]{:S(2)}) copy-start(bf16[34,1,384]{2,1,0:T(2,128)(2,1)S(1)} %collective-permute-done.2.refs_1_) | copy-start | bytes 78340
  89.2 0.6 copy-start.18

commit v4 on v3

--- a/solution.py
+++ b/solution.py
@@ -50,7 +50,7 @@
         )
 
     acc = lax.fori_loop(
-        0, loaders // together, add, jnp.zeros((tile, channels), F32), unroll=2
+        0, loaders // together, add, jnp.zeros((tile, channels), F32), unroll=4
     )
     grid_ref[...] = acc.astype(BF)
     normed = rms(acc, gain_ref[...]).astype(BF)
@@ -395,7 +395,7 @@
             sum_ref[:, here, at] = y_ref[:, here, at] + block.reshape(rows_n, GROUP, LANES)
         return carry
 
-    lax.fori_loop(0, cols_n // GROUP, one_group, 0)
+    lax.fori_loop(0, cols_n // GROUP, one_group, 0, unroll=2)
 
     def some_rows(s, carry):
         for i in range(span):

time: 192 us -> 190 us (0.990)
  Pallas kernels: 120 us -> 118 us
where the time goes in v4:
time: 190 us; the launch traced here: 189 us
  Pallas kernels  118 us (62%)
  local copies, waits for them, and re-layouts  26.7 us (14%)
  starting transfers between devices  14 us (7%)
  other arithmetic  13.3 us (7%)
  waiting for transfers between devices  12.8 us (7%)
  matrix products  4.01 us (2%)
    pallas_call x2, Pallas kernels, call(): pl.pallas_call(kernel, in_specs=[VMEM] * len(args), out_specs=[pl.BlockSp...  99.8 us
    pallas_call x1, Pallas kernels, place(): pl.pallas_call(place_kernel, grid=(n_cells // tile,), in_specs=[whole(val...  18.1 us
    all_to_all x1, starting transfers between devices, local(): lax.all_to_all(sent, ('row', 'col'), split_axis=1, concat_axis=0, tiled=T...  7.3 us
    all_to_all x1, waiting for transfers between devices, local(): lax.all_to_all(sent, ('row', 'col'), split_axis=1, concat_axis=0, tiled=T...  7.14 us
    ppermute x2, waiting for transfers between devices, halo(): high = lax.ppermute(lax.slice_in_dim(block, 0, 1, axis=dim), axis, backward)  5.65 us
    unnamed x51, local copies, waits for them, and re-layouts  4.8 us
    ppermute x2, starting transfers between devices, halo(): lax.ppermute(lax.slice_in_dim(block, n - 1, n, axis=dim), axis, forward)  4.14 us
    reshape x2, local copies, waits for them, and re-layouts, rate_vectors(): return (vecs, jnp.swapaxes(cum.reshape(both), 1, 2), decay)  3.94 us
  transfers between devices with their start and end apart: 5, of which 3 were waited for; matrix products, arithmetic and copies ran while one was open for 18% of the time, Pallas kernels for 0%

profile of v4, /device:TPU:0, one launch (start us, length us, event | category | flops | bytes accessed | tf_op | source)
XLA Modules:
  0.0 189.3 jit_solution(14321660243841101480)
XLA Ops:
  0.0 0.8 fusion.57
  0.9 0.7 compare_bitcast_fusion
  1.6 1.6 bitcast_select_fusion
  3.2 1.3 pad_maximum_fusion.1
  4.5 7.3 %all-to-all-start = ((bf16[1,32,128,194]{2,3,0,1:T(8,128)(2,1)}), bf16[1,32,128,194]{2,3,0,1:T(8,128)(2,1)S(1)}, u32[]{:S(2)}, u32[]{:S(2)}) async-start(bf16[1,32,128,194]{2,3,0,1:T(8,128)(2,1)} %pad_maximum_fusion.1), calls=%async_computation | async-start | bytes 3276800 | tf_op jit(solution)/shard_map/all_to_all | solution.py:494
  11.8 0.2 fusion.30
  12.1 0.7 fusion.70
  12.8 1.2 copy.192
  13.9 1.7 copy.164
  15.6 1.4 fusion.33
  17.0 0.7 broadcast_in_dim.51
  17.7 1.4 reshape.359
  19.1 0.8 reshape.356
  19.9 1.3 copy.167
  21.2 0.8 copy.237
  22.0 1.4 fusion
  23.4 0.0 copy-done.3
  23.4 1.1 bitcast_add_fusion
  24.5 0.1 copy.169
  24.5 0.1 copy.174
  24.7 0.1 copy.172
  24.7 0.8 copy.175
  25.6 0.1 copy.173
  25.6 0.8 copy.176
  26.4 0.2 fusion.39
  26.7 0.1 copy.238
  26.8 0.2 fusion.37
  27.1 1.2 bitcast_add_fusion.1
  28.3 0.8 copy.156
  29.2 0.8 copy.157
  30.1 0.8 copy.158
  30.9 2.0 %copy.178 = f32[16,12,256]{1,2,0:T(8,128)} copy(f32[16,12,256]{2,0,1:T(8,128)S(1)} %bitcast.142) | data formatting | bytes 393216 | tf_op jit(solution)/shard_map/reshape | solution.py:464
  32.9 2.0 %copy.160 = f32[32,12,128]{1,2,0:T(8,128)} copy(f32[32,12,128]{2,0,1:T(8,128)S(1)} %bitcast.141) | data formatting | bytes 393216 | tf_op jit(solution)/shard_map/reshape | solution.py:464
  34.9 0.2 copy.161
  35.1 0.6 reshape.351.refs_3_
  35.7 0.5 broadcast_in_dim.53.refs_4_
  36.2 0.6 broadcast_in_dim.54.refs_10_
  36.8 0.9 copy.181.ff_out_ref
  37.8 0.8 copy.180.out_w_ref
  38.6 0.5 broadcast_in_dim.55.gain_ref
  39.2 0.3 fusion.55
  39.5 0.1 reshape_bitcast_fusion
  39.5 1.7 pad_maximum_fusion.4.w_ref
  41.3 0.9 slice_bitcast_fusion.2
  42.2 1.1 pad_maximum_fusion.3.refs_7_.cv_ref
  43.3 1.1 pad_maximum_fusion.2.refs_6_.rv_ref
  44.4 0.5 convolution_bitcast_fusion
  44.9 7.1 %all-to-all-done = bf16[1,32,128,194]{2,3,0,1:T(8,128)(2,1)S(1)} async-done(((bf16[1,32,128,194]{2,3,0,1:T(8,128)(2,1)}), bf16[1,32,128,194]{2,3,0,1:T(8,128)(2,1)S(1)}, u32[]{:S(2)}, u32[]{:S(2)}) %all-to-all-start) | async-done | bytes 1589280 | tf_op jit(solution)/shard_map/all_to_all | solution.py:494
  52.1 1.2 copy-done.1
  53.2 18.1 %place.1 = (bf16[4096,192]{1,0:T(8,128)(2,1)}, bf16[4096,384]{1,0:T(8,128)(2,1)}, bf16[4096,384]{1,0:T(8,128)(2,1)}) custom-call(bf16[32,194,128]{2,1,0:T(8,128)(2,1)} %bitcast.136, f32[1,192]{1,0:T(1,128)} %bitcast.152, bf16[192,768]{1,0:T(8,128)(2,1)} %pad_maximum_fusion.4.w_ref), custom_call_target="tpu_custom_call" | custom-call | tf_op jit(solution)/shard_map/place/pallas_call | solution.py:73
  71.3 1.0 slice_bitcast_fusion.5
  72.3 1.6 collective-permute-start
  73.9 1.3 collective-permute-start.1
  75.2 0.8 slice_bitcast_fusion
  75.9 1.6 collective-permute-done.1
  77.6 2.4 %pad_maximum_fusion.refs_0_ = bf16[34,128,384]{2,1,0:T(8,128)(2,1)S(1)} fusion(bf16[1,128,384]{2,1,0:T(8,128)(2,1)S(1)} %collective-permute-done.1, bf16[32,128,384]{2,1,0:T(8,128)(2,1)} %bitcast.137, bf16[1,128,384]{2,1,0:T(8,128)(2,1)S(1)} %collective-permute-done), kind=kLoop, calls=%fused_computation | loop fusion | flops 3342336 | bytes 6684672 | tf_op jit(solution)/shard_map/concatenate | solution.py:513
  80.0 0.1 fusion.69
  80.1 2.6 %collective-permute-start.2 = (bf16[34,1,384]{2,1,0:T(2,128)(2,1)S(1)}, bf16[34,1,384]{2,1,0:T(2,128)(2,1)S(1)}, u32[]{:S(2)}, u32[]{:S(2)}) collective-permute-start(bf16[34,1,384]{2,1,0:T(2,128)(2,1)S(1)} %get-tuple-element.40), channel_id=1, source_target_pairs={{0,1},{1,2},{2,3},{3,4},{4,5},{5,6},{6,7},{8,9},{9,10},{10,11},{11... | collective-permute-start | bytes 78344 | tf_op jit(solution)/shard_map/ppermute | solution.py:472
  82.6 1.3 collective-permute-start.3
  83.9 0.7 slice_bitcast_fusion.6
  84.6 4.0 %collective-permute-done.3.refs_2_ = bf16[34,1,384]{2,1,0:T(2,128)(2,1)S(1)} collective-permute-done((bf16[34,1,384]{2,1,0:T(2,128)(2,1)S(1)}, bf16[34,1,384]{2,1,0:T(2,128)(2,1)S(1)}, u32[]{:S(2)}, u32[]{:S(2)}) %collective-permute-start.3) | collective-permute-done | bytes 26144 | tf_op jit(solution)/shard_map/ppermute | solution.py:473
  88.7 0.6 copy-done.18
  89.3 75.6 %conv_scan.1 = (f32[32,128,384]{2,1,0:T(8,128)}, bf16[32,128,128]{2,1,0:T(8,128)(2,1)}, bf16[16,128,256]{2,1,0:T(8,128)(2,1)}, bf16[32,16,384]{2,1,0:T(8,128)(2,...) custom-call(bf16[34,128,384]{2,1,0:T(8,128)(2,1)} %copy-done, ...), custom_call_target="tpu_custom_call" | custom-call | tf_op jit(solution)/shard_map/conv_scan/pallas_call | solution.py:433
  164.9 24.2 %finish.1 = bf16[32,192,128]{2,1,0:T(8,128)(2,1)} custom-call(f32[32,128,384]{2,1,0:T(8,128)} %get-tuple-element.30.y_ref, bf16[32,128,128]{2,1,0:T(8,128)(2,1)} %get-tuple-element.31.rc_ref, bf16[16,128,256]{2,1,0:T(8,128)(2,1)} %get-tuple-element.32.cc_ref, f32[32,42,128]{2,1,0:T(8,128)} %pad_maximum_fusion.2.refs_6_.rv_ref, ...), custom_call_target="tpu_custom_call" | custom-call | tf_op jit(solution)/shard_map/finish/pallas_call | solution.py:433
  (56 shorter events, 0.3 us)
Async XLA Ops:
  4.5 7.5 %copy-start.4 = (f32[4,6,32,128]{3,2,1,0:T(8,128)S(1)}, f32[4,6,32,128]{3,2,1,0:T(8,128)}, u32[]{:S(2)}) copy-start(f32[4,6,32,128]{3,2,1,0:T(8,128)} %param.30) | copy-start | bytes 1179652
  4.5 47.6 %all-to-all-start = ((bf16[1,32,128,194]{2,3,0,1:T(8,128)(2,1)}), bf16[1,32,128,194]{2,3,0,1:T(8,128)(2,1)S(1)}, u32[]{:S(2)}, u32[]{:S(2)}) async-start(bf16[1,32,128,194]{2,3,0,1:T(8,128)(2,1)} %pad_maximum_fusion.1), calls=%async_computation | async-start | bytes 3276800 | tf_op jit(solution)/shard_map/all_to_all | solution.py:494
  17.0 5.0 %copy-start.2 = (f32[256,16,2,6]{0,1,3,2:T(8,128)}, f32[256,16,2,6]{0,1,3,2:T(8,128)S(1)}, u32[]{:S(2)}) copy-start(f32[256,16,2,6]{0,1,3,2:T(8,128)S(1)} %fusion.33) | copy-start | bytes 589828
  21.2 2.2 %copy-start.6 = (f32[16,2,6,256]{3,2,0,1:T(8,128)S(1)}, f32[16,2,6,256]{3,2,0,1:T(8,128)}, u32[]{:S(2)}) copy-start(f32[16,2,6,256]{3,2,0,1:T(8,128)} %copy.167) | copy-start | bytes 589828
  22.0 1.4 copy-start.3
  24.5 2.0 %copy-start.5 = (f32[4,6,32,128]{3,2,1,0:T(8,128)S(1)}, f32[4,6,32,128]{3,2,1,0:T(8,128)}, u32[]{:S(2)}) copy-start(f32[4,6,32,128]{3,2,1,0:T(8,128)} %param.30) | copy-start | bytes 1179652
  24.7 2.4 %copy-start.12 = (f32[2,6,32,128]{3,2,1,0:T(8,128)S(1)}, f32[2,6,32,128]{3,2,1,0:T(8,128)}, u32[]{:S(2)}) copy-start(f32[2,6,32,128]{3,2,1,0:T(8,128)} %get-tuple-element.48) | copy-start | bytes 589828
  32.9 2.2 %copy-start.20 = (f32[3,3,384]{2,1,0:T(4,128)S(1)}, f32[3,3,384]{2,1,0:T(4,128)}, u32[]{:S(2)}) copy-start(f32[3,3,384]{2,1,0:T(4,128)} %param.26) | copy-start | bytes 41476
  32.9 2.8 %copy-start.21 = (f32[384]{0:T(512)S(1)}, f32[384]{0:T(512)}, u32[]{:S(2)}) copy-start(f32[384]{0:T(512)} %param.27) | copy-start | bytes 4612
  32.9 3.4 %copy-start.22 = (f32[384]{0:T(512)S(1)}, f32[384]{0:T(512)}, u32[]{:S(2)}) copy-start(f32[384]{0:T(512)} %param.29) | copy-start | bytes 4612
  32.9 4.0 %copy-start.15 = (bf16[768,192]{0,1:T(8,128)(2,1)S(1)}, bf16[768,192]{0,1:T(8,128)(2,1)}, u32[]{:S(2)}) copy-start(bf16[768,192]{0,1:T(8,128)(2,1)} %param.35) | copy-start | bytes 884740
  32.9 4.9 %copy-start.16 = (bf16[384,192]{0,1:T(8,128)(2,1)S(1)}, bf16[384,192]{0,1:T(8,128)(2,1)}, u32[]{:S(2)}) copy-start(bf16[384,192]{0,1:T(8,128)(2,1)} %param.32) | copy-start | bytes 442372
  32.9 5.7 %copy-start.23 = (f32[384]{0:T(512)S(1)}, f32[384]{0:T(512)}, u32[]{:S(2)}) copy-start(f32[384]{0:T(512)} %param.31) | copy-start | bytes 4612
  34.9 7.3 %copy-start.7 = (f32[16,12,256]{2,1,0:T(8,128)S(1)}, f32[16,12,256]{2,1,0:T(8,128)}, u32[]{:S(2)}) copy-start(f32[16,12,256]{2,1,0:T(8,128)} %copy.175) | copy-start | bytes 589828
  34.9 7.3 %copy-start.8 = (f32[16,12,256]{2,1,0:T(8,128)S(1)}, f32[16,12,256]{2,1,0:T(8,128)}, u32[]{:S(2)}) copy-start(f32[16,12,256]{2,1,0:T(8,128)} %copy.176) | copy-start | bytes 589828
  37.8 5.5 %copy-start.13 = (f32[32,2,6,128]{3,2,0,1:T(8,128)S(1)}, f32[32,2,6,128]{3,2,0,1:T(8,128)}, u32[]{:S(2)}) copy-start(f32[32,2,6,128]{3,2,0,1:T(8,128)} %get-tuple-element.53) | copy-start | bytes 589828
  38.6 4.7 %copy-start.9 = (f32[32,12,128]{2,1,0:T(8,128)S(1)}, f32[32,12,128]{2,1,0:T(8,128)}, u32[]{:S(2)}) copy-start(f32[32,12,128]{2,1,0:T(8,128)} %copy.156) | copy-start | bytes 589828
  38.6 4.7 %copy-start.10 = (f32[32,12,128]{2,1,0:T(8,128)S(1)}, f32[32,12,128]{2,1,0:T(8,128)}, u32[]{:S(2)}) copy-start(f32[32,12,128]{2,1,0:T(8,128)} %copy.157) | copy-start | bytes 589828
  38.6 4.7 %copy-start.11 = (f32[32,12,128]{2,1,0:T(8,128)S(1)}, f32[32,12,128]{2,1,0:T(8,128)}, u32[]{:S(2)}) copy-start(f32[32,12,128]{2,1,0:T(8,128)} %copy.158) | copy-start | bytes 589828
  42.2 2.2 %copy-start.14 = (f32[256,16,2,6]{0,3,1,2:T(8,128)S(1)}, f32[256,16,2,6]{0,3,1,2:T(8,128)}, u32[]{:S(2)}) copy-start(f32[256,16,2,6]{0,3,1,2:T(8,128)} %copy.237) | copy-start | bytes 589828
  42.2 2.2 %copy-start.19 = (f32[6,384,1,1]{1,0,2,3:T(8,128)S(1)}, f32[6,384,1,1]{1,0,2,3:T(8,128)}, u32[]{:S(2)}) copy-start(f32[6,384,1,1]{1,0,2,3:T(8,128)} %reshape.359) | copy-start | bytes 27652
  52.1 1.2 copy-start.1
  72.3 3.6 %collective-permute-start = (bf16[1,128,384]{2,1,0:T(8,128)(2,1)S(1)}, bf16[1,128,384]{2,1,0:T(8,128)(2,1)S(1)}, u32[]{:S(2)}, u32[]{:S(2)}) collective-permute-start(bf16[1,128,384]{2,1,0:T(8,128)(2,1)S(1)} %get-tuple-element.41), channel_id=1, source_target_pairs={{0,8},{8,16},{16,24},{1,9},{9,17},{17,25},{2,10},{10,18},{18,26},{... | collective-permute-start | bytes 294920 | tf_op jit(solution)/shard_map/ppermute | solution.py:472
  73.9 3.7 %collective-permute-start.1 = (bf16[1,128,384]{2,1,0:T(8,128)(2,1)S(1)}, bf16[1,128,384]{2,1,0:T(8,128)(2,1)S(1)}, u32[]{:S(2)}, u32[]{:S(2)}) collective-permute-start(bf16[1,128,384]{2,1,0:T(8,128)(2,1)S(1)} %get-tuple-element.42), channel_id=1, source_target_pairs={{8,0},{16,8},{24,16},{9,1},{17,9},{25,17},{10,2},{18,10},{26,18},{... | collective-permute-start | bytes 294920 | tf_op jit(solution)/shard_map/ppermute | solution.py:473
  80.0 8.7 %copy-start = (bf16[34,128,384]{2,1,0:T(8,128)(2,1)}, bf16[34,128,384]{2,1,0:T(8,128)(2,1)S(1)}, u32[]{:S(2)}) copy-start(bf16[34,128,384]{2,1,0:T(8,128)(2,1)S(1)} %pad_maximum_fusion.refs_0_) | copy-start | bytes 10027012
  80.1 4.6 %collective-permute-start.2 = (bf16[34,1,384]{2,1,0:T(2,128)(2,1)S(1)}, bf16[34,1,384]{2,1,0:T(2,128)(2,1)S(1)}, u32[]{:S(2)}, u32[]{:S(2)}) collective-permute-start(bf16[34,1,384]{2,1,0:T(2,128)(2,1)S(1)} %get-tuple-element.40), channel_id=1, source_target_pairs={{0,1},{1,2},{2,3},{3,4},{4,5},{5,6},{6,7},{8,9},{9,10},{10,11},{11... | collective-permute-start | bytes 78344 | tf_op jit(solution)/shard_map/ppermute | solution.py:472
  82.6 6.0 %collective-permute-start.3 = (bf16[34,1,384]{2,1,0:T(2,128)(2,1)S(1)}, bf16[34,1,384]{2,1,0:T(2,128)(2,1)S(1)}, u32[]{:S(2)}, u32[]{:S(2)}) collective-permute-start(bf16[34,1,384]{2,1,0:T(2,128)(2,1)S(1)} %get-tuple-element.39), channel_id=1, source_target_pairs={{1,0},{2,1},{3,2},{4,3},{5,4},{6,5},{7,6},{9,8},{10,9},{11,10},{12... | collective-permute-start | bytes 78344 | tf_op jit(solution)/shard_map/ppermute | solution.py:473
  84.6 4.0 %copy-start.17 = (bf16[34,1,384]{2,1,0:T(2,128)(2,1)}, bf16[34,1,384]{2,1,0:T(2,128)(2,1)S(1)}, u32[]{:S(2)}) copy-start(bf16[34,1,384]{2,1,0:T(2,128)(2,1)S(1)} %collective-permute-done.2.refs_1_) | copy-start | bytes 78340
  88.7 0.6 copy-start.18
